TPU v7x, 32 devices: a whole 2x2x4 slice. The times are simulated.
32 devices in a mesh: gx: 4 (over x, core), gy: 2 (over y), gz: 4 (over z).
Axes of the slice: x: 2, y: 2, z: 4, core: 2. Of those that a mesh axis runs over, the one named last changes fastest.
Arguments:
- state: float32 [4, 96, 128, 512], P(None, 'gz', 'gx', 'gy'), may hold values from -5 to 5
- mixing: float32 [2, 96, 128, 512], P(None, 'gz', 'gx', 'gy'), may hold values from 0.1 to 1000
- depth_levels: int32 [128, 512], replicated, may hold values from 0 to 96
- wind: float32 [2, 128, 512], P(None, 'gx', 'gy'), may hold values from -3 to 3
Outputs:
- state_next: float32 [4, 96, 128, 512], P(None, 'gz', 'gx', 'gy')
Inputs may be any that keep to these rules, and one draw needn't show every extreme that they name: `depth_levels`: levels at or beyond a column's count are land.
All inputs are finite; a program needn't handle non-finite values.
Results may differ from a plain program's by a relative error of at most 0.0003.
Values sent between devices are 32-bit elements; how exact they have to be, the bound alone decides.
A program may use at most 192 MiB of HBM per device.

v0:
```python
import jax
import jax.numpy as jnp
from jax import lax
from jax.sharding import PartitionSpec as P


def padded_2(array, sides, width):
    for axis, dim in sides:
        peers, length = (lax.axis_size(axis), array.shape[dim])
        up = [(i, (i + 1) % peers) for i in range(peers)]
        down = [(j, i) for i, j in up]
        last = lax.slice_in_dim(array, length - width, length, axis=dim)
        initial = lax.slice_in_dim(array, 0, width, axis=dim)
        before = lax.ppermute(last, axis, up)
        after = lax.ppermute(initial, axis, down)
        array = jnp.concatenate([before, array, after], axis=dim)
    return array


def carried_in(part, axis, combine, identity):
    place = lax.axis_index(axis)
    gathered = lax.all_gather(part, axis)
    state = jnp.zeros_like(part) + jnp.asarray(identity, part.dtype)

    def one(turn, state):
        return combine(state, lax.dynamic_index_in_dim(gathered, turn, 0, False))

    return lax.fori_loop(0, place, one, state)


def density_of(fields, wet_mask):
    return (-0.3 * fields[0] + 0.7 * fields[1] - 0.05 * fields[0] * fields[0]) * wet_mask


def advance(padded, wet_pad, pressure, wall_face, coriolis):
    wet_x = wet_pad[:, :-1, 1:-1] * wet_pad[:, 1:, 1:-1]
    wet_y = wet_pad[:, 1:-1, :-1] * wet_pad[:, 1:-1, 1:] * wall_face
    east_vel = 0.5 * (padded[2, :, :-1, 1:-1] + padded[2, :, 1:, 1:-1]) * wet_x
    north_vel = 0.5 * (padded[3, :, 1:-1, :-1] + padded[3, :, 1:-1, 1:]) * wet_y
    west_side = padded[:, :, :-1, 1:-1]
    east_side = padded[:, :, 1:, 1:-1]
    flux_x = 0.25 * (
        jnp.maximum(east_vel, 0.0) * west_side + jnp.minimum(east_vel, 0.0) * east_side
    ) - 0.08 * wet_x * (east_side - west_side)
    south_side = padded[:, :, 1:-1, :-1]
    north_side = padded[:, :, 1:-1, 1:]
    flux_y = 0.25 * (
        jnp.maximum(north_vel, 0.0) * south_side + jnp.minimum(north_vel, 0.0) * north_side
    ) - 0.08 * wet_y * (north_side - south_side)
    interior = padded[:, :, 1:-1, 1:-1]
    moved = interior - (
        flux_x[:, :, 1:] - flux_x[:, :, :-1] + flux_y[:, :, :, 1:] - flux_y[:, :, :, :-1]
    )
    centre = pressure[:, 1:-1, 1:-1]
    grad_x = 0.5 * (
        wet_x[:, 1:] * (pressure[:, 2:, 1:-1] - centre)
        + wet_x[:, :-1] * (centre - pressure[:, :-2, 1:-1])
    )
    grad_y = 0.5 * (
        wet_y[:, :, 1:] * (pressure[:, 1:-1, 2:] - centre)
        + wet_y[:, :, :-1] * (centre - pressure[:, 1:-1, :-2])
    )
    east_new = moved[2] + 0.3 * coriolis * interior[3] - grad_x
    north_new = moved[3] - 0.3 * coriolis * interior[2] - grad_y
    wet_inner = wet_pad[:, 1:-1, 1:-1]
    return jnp.stack([moved[0], moved[1], east_new, north_new]) * wet_inner


def thomas(rhs_lev, below_lev, above_lev):

    def forward(carry, item):
        ratio_prev, value_prev = carry
        rhs_here, below_here, above_here = item
        divisor = 1.0 + above_here * (1.0 - ratio_prev) + below_here
        ratio = below_here / divisor
        value = (rhs_here + above_here * value_prev) / divisor
        return ((ratio, value), (ratio, value))

    zero_level = jnp.zeros_like(rhs_lev[0])
    ratio_start = jnp.zeros_like(below_lev[0] * rhs_lev[0])
    _, (ratios, values) = lax.scan(
        forward, (ratio_start, zero_level), (rhs_lev, below_lev, above_lev), unroll=8
    )

    def backward(later, item):
        ratio, value = item
        result = value + ratio * later
        return (result, result)

    _, solved = lax.scan(backward, zero_level, (ratios, values), reverse=True, unroll=8)
    return solved


def tridiagonal(forced, coupling):
    below = jnp.repeat(coupling, 2, axis=0)
    above = jnp.concatenate([jnp.zeros_like(below[:, :1]), below[:, :-1]], axis=1)
    solved = thomas(
        jnp.moveaxis(forced, 1, 0), jnp.moveaxis(below, 1, 0), jnp.moveaxis(above, 1, 0)
    )
    return jnp.moveaxis(solved, 0, 1)


def add_totals(earlier, later):
    return earlier + later


def per_device(state, mixing, depth_levels, wind):
    fields, lev_count, col_x, col_y = state.shape
    total_x, total_y = depth_levels.shape
    start_x = lax.axis_index("gx") * col_x
    start_y = lax.axis_index("gy") * col_y
    start_z = lax.axis_index("gz") * lev_count
    padded = padded_2(state, (("gx", 2), ("gy", 3)), 1)
    row_index = (start_x - 1 + jnp.arange(col_x + 2, dtype=jnp.int32)) % total_x
    col_index = (start_y - 1 + jnp.arange(col_y + 2, dtype=jnp.int32)) % total_y
    depth_pad = jnp.take(jnp.take(depth_levels, row_index, axis=0), col_index, axis=1)
    levels = start_z + jnp.arange(lev_count, dtype=jnp.int32)
    wet_pad = (levels[:, None, None] < depth_pad[None]).astype(jnp.float32)
    density_field = density_of(padded, wet_pad)
    inclusive = jnp.cumsum(density_field, axis=0)
    column_total = inclusive[-1]
    shallower = carried_in(column_total, "gz", add_totals, jnp.zeros_like(column_total))
    pressure = 0.03 * (shallower[None] + inclusive - 0.5 * density_field)
    face_row = start_y - 1 + jnp.arange(col_y + 1, dtype=jnp.int32)
    wall_face = ((face_row >= 0) & (face_row <= total_y - 2)).astype(jnp.float32)
    row_global = start_y + jnp.arange(col_y, dtype=jnp.int32)
    coriolis = 0.5 + (row_global.astype(jnp.float32) + 0.5) / total_y
    forced = advance(padded, wet_pad, pressure, wall_face, coriolis)
    wet_inner = wet_pad[:, 1:-1, 1:-1]
    depth_inner = depth_pad[1:-1, 1:-1]
    wet_next = ((levels + 1)[:, None, None] < depth_inner[None]).astype(jnp.float32)
    top_level = (levels == 0).astype(jnp.float32)
    forced = forced.at[2:].add(wind[:, None] * top_level[None, :, None, None] * wet_inner[None])
    coupling = mixing * (wet_inner * wet_next)[None]
    whole_forced, whole_coupling = (
        lax.all_gather(forced, "gz", axis=1, tiled=True),
        lax.all_gather(coupling, "gz", axis=1, tiled=True),
    )
    solved = tridiagonal(whole_forced, whole_coupling)
    result = lax.dynamic_slice_in_dim(solved, start_z, lev_count, 1)
    return result


def solution(mesh):
    return jax.shard_map(
        per_device,
        mesh=mesh,
        in_specs=(P(None, "gz", "gx", "gy"), P(None, "gz", "gx", "gy"), P(), P(None, "gx", "gy")),
        out_specs=P(None, "gz", "gx", "gy"),
        check_vma=False,
    )
```

profile of v0, /device:TPU:0, one launch (start us, length us, event | category | flops | bytes accessed | tf_op | source)
XLA Modules:
  0.0 549.4 jit_solution(16116721438880456935)
XLA Ops:
  12.3 2.9 broadcast_multiply_fusion
  16.6 1.9 collective-permute-start.1
  19.1 1.9 constant_dynamic-update-slice_fusion
  22.3 2.6 fusion.103
  24.8 2.5 copy.21
  27.4 2.4 collective-permute-start.2
  29.8 2.3 copy.23
  32.4 2.8 dynamic-update-slice.28
  35.1 2.7 broadcast_maximum_fusion.1
  40.4 2.9 multiply_subtract_fusion.1
  43.3 2.1 copy.22
  45.4 2.9 copy.24
  48.3 3.1 compare_select_fusion
  51.4 5.1 fusion.106
  58.6 2.9 multiply_subtract_fusion
  61.5 3.1 fusion.43
  65.4 21.6 %all_gather.10 = f32[4,34,258]{2,1,0:T(8,128)} all-gather(f32[1,34,258]{2,1,0:T(8,128)S(1)} %slice-done.1), channel_id=1, replica_groups=mesh['gx'=4,'gy'=2,'gz'=4] {'gz'}, dimensions={0}, use_global_device_ids=true | all-gather | bytes 175440 | tf_op jit(solution)/shard_map/all_gather | solution.py:22
  87.1 2.2 subtract_multiply_fusion
  89.6 2.6 fusion.69
  93.5 1.7 copy-done.8
  95.2 42.2 %all-gather.3.cloned.1.call-done = f32[2,96,32,256]{3,2,1,0:T(8,128)} async-done(((f32[2,24,32,256]{3,2,1,0:T(8,128)}), f32[2,96,32,256]{3,2,1,0:T(8,128)}) %all-gather.3.cloned.1.call-update) | async-done | bytes 6291472 | tf_op jit(solution)/shard_map/all_gather | solution.py:137
  137.4 3.9 copy.20
  141.3 8.2 %broadcast_in_dim.186 = f32[2,2,96,32,256]{4,3,1,0,2:T(8,128)} broadcast(f32[2,96,32,256]{3,2,0,1:T(8,128)S(1)} %copy.20), dimensions={0,2,3,4} | broadcast | bytes 18874368 | tf_op jit(solution)/shard_map/broadcast_in_dim | solution.py:95
  149.5 12.7 %slice.499 = f32[4,95,32,256]{3,2,0,1:T(8,128)} slice(f32[4,96,32,256]{3,2,0,1:T(8,128)} %bitcast.484), slice={[0:4], [0:95], [0:32], [0:256]} | slice | bytes 24903680 | tf_op jit(solution)/shard_map/slice | solution.py:96
  162.2 11.9 %concatenate.42 = f32[4,96,32,256]{3,2,0,1:T(8,128)} pad(f32[4,95,32,256]{3,2,0,1:T(8,128)} %slice.499, f32[]{:T(128)} %constant.186.clone.1), padding=0_0x1_0x0_0x0_0 | pad | bytes 25034756 | tf_op jit(solution)/shard_map/concatenate | solution.py:96
  174.1 181.2 %all-gather.5.cloned.1.call-done = f32[4,96,32,256]{3,2,1,0:T(8,128)} async-done(((f32[4,24,32,256]{3,2,1,0:T(8,128)}), f32[4,96,32,256]{3,2,1,0:T(8,128)}) %all-gather.5.cloned.1.call-update) | async-done | bytes 12582928 | tf_op jit(solution)/shard_map/all_gather | solution.py:136
  355.4 141.2 %while.46 = (s32[]{:T(128)}, f32[4,32,256]{2,1,0:T(8,128)S(1)}, f32[4,32,256]{2,1,0:T(8,128)S(1)}, f32[12,8,4,32,256]{4,3,2,1,0:T(8,128)}, f32[12,8,4,32,256]{4,...) while((s32[]{:T(128)}, f32[4,32,256]{2,1,0:T(8,128)S(1)}, ...), condition=%wide.region_4.5_spmd.clone, body=%wide.region_3.4_spmd.clone.sunk | while | flops 2162696 | bytes 14943063 | solution.py:81
  400.9 1.5 bitcast_dynamic-update-slice_fusion.53
  412.7 1.5 bitcast_dynamic-update-slice_fusion.53
  424.5 1.5 bitcast_dynamic-update-slice_fusion.53
  436.3 1.5 bitcast_dynamic-update-slice_fusion.53
  459.9 1.5 bitcast_dynamic-update-slice_fusion.53
  483.4 1.5 bitcast_dynamic-update-slice_fusion.53
  496.6 6.2 %broadcast.313.clone = f32[12,8,4,32,256]{4,3,1,0,2:T(8,128)} broadcast(f32[]{:T(128)} %constant.186.clone.1), dimensions={} | broadcast | bytes 12582916 | tf_op jit(solution)/shard_map/broadcast.15
  502.8 35.7 %while.47 = (s32[]{:T(128)}, f32[4,32,256]{2,1,0:T(8,128)S(1)}, f32[12,8,4,32,256]{4,3,1,0,2:T(8,128)}, f32[12,8,4,32,256]{4,3,2,1,0:T(8,128)}, f32[12,8,4,32,25...) while((s32[]{:T(128)}, f32[4,32,256]{2,1,0:T(8,128)S(1)}, ...), condition=%wide.region_6.7_spmd.clone, body=%wide.region_5.6_spmd.clone.sunk | while | flops 557066 | bytes 7340315 | solution.py:90
  502.8 1.8 bitcast_dynamic-update-slice_fusion.54
  505.7 1.8 bitcast_dynamic-update-slice_fusion.54
  508.8 1.8 bitcast_dynamic-update-slice_fusion.54
  511.7 1.8 bitcast_dynamic-update-slice_fusion.54
  514.7 1.8 bitcast_dynamic-update-slice_fusion.54
  517.7 1.8 bitcast_dynamic-update-slice_fusion.54
  520.6 1.8 bitcast_dynamic-update-slice_fusion.54
  523.6 1.8 bitcast_dynamic-update-slice_fusion.54
  526.5 1.8 bitcast_dynamic-update-slice_fusion.54
  529.5 1.8 bitcast_dynamic-update-slice_fusion.54
  532.5 1.8 bitcast_dynamic-update-slice_fusion.54
  535.5 1.8 bitcast_dynamic-update-slice_fusion.54
  538.5 4.0 dynamic-slice_bitcast_fusion.40
  (302 shorter events, 161.3 us)
Async XLA Ops:
  6.5 1.0 copy-start
  6.5 130.9 %all-gather.3.cloned.1.call-start = ((), (), s32[]{:S(2)}) async-start(), calls=%async_computation | async-start | bytes 7864320 | tf_op jit(solution)/shard_map/all_gather | solution.py:137
  9.7 5.5 %copy-start.18 = (s32[24]{0:T(128)}, s32[24]{0:T(128)S(1)}, u32[]{:S(2)}) copy-start(s32[24]{0:T(128)S(1)} %iota_add_fusion.1) | copy-start | bytes 292
  10.0 1.1 copy-start.5
  12.3 3.0 copy-start.2
  15.3 340.1 %all-gather.5.cloned.1.call-start = ((), (), s32[]{:S(2)}) async-start(), calls=%async_computation.1 | async-start | bytes 15728640 | tf_op jit(solution)/shard_map/all_gather | solution.py:136
  16.1 5.4 collective-permute-start
  16.6 5.0 collective-permute-start.1
  27.4 15.9 %collective-permute-start.2 = (f32[4,24,34,1]{2,1,3,0:T(8,128)S(1)}, f32[4,24,34,1]{2,1,3,0:T(8,128)S(1)}, u32[]{:S(2)}, u32[]{:S(2)}) collective-permute-start(f32[4,24,34,1]{2,1,3,0:T(8,128)S(1)} %copy.21), channel_id=1, source_target_pairs={{0,4},{4,0},{1,5},{5,1},{2,6},{6,2},{3,7},{7,3},{8,12},{12,8},{9,1... | collective-permute-start | bytes 39176 | tf_op jit(solution)/shard_map/ppermute | solution.py:14
  32.1 13.3 %collective-permute-start.3 = (f32[4,24,34,1]{2,1,3,0:T(8,128)S(1)}, f32[4,24,34,1]{2,1,3,0:T(8,128)}, u32[]{:S(2)}, u32[]{:S(2)}) collective-permute-start(f32[4,24,34,1]{2,1,3,0:T(8,128)S(1)} %copy.23), channel_id=1, source_target_pairs={{4,0},{0,4},{5,1},{1,5},{6,2},{2,6},{7,3},{3,7},{12,8},{8,12},{13,... | collective-permute-start | bytes 39176 | tf_op jit(solution)/shard_map/ppermute | solution.py:15
  37.9 1.0 copy-start.13
  37.9 2.5 copy-start.9
  43.3 5.0 copy-start.19
  48.3 8.2 %copy-start.4 = (f32[4,24,34,1]{3,2,1,0:T(8,128)S(1)}, f32[4,24,34,1]{3,2,1,0:T(8,128)}, u32[]{:S(2)}) copy-start(f32[4,24,34,1]{3,2,1,0:T(8,128)} %copy.24) | copy-start | bytes 39172
  48.3 8.2 %copy-start.6 = (f32[24,34,258]{2,1,0:T(8,128)S(1)}, f32[24,34,258]{2,1,0:T(8,128)}, u32[]{:S(2)}) copy-start(f32[24,34,258]{2,1,0:T(8,128)} %copy-done.5) | copy-start | bytes 2526340
  51.4 6.1 %copy-start.10 = (f32[24,34,258]{2,1,0:T(8,128)}, f32[24,34,258]{2,1,0:T(8,128)S(1)}, u32[]{:S(2)}) copy-start(f32[24,34,258]{2,1,0:T(8,128)S(1)} %compare_select_fusion) | copy-start | bytes 2526340
  51.4 5.1 copy-start.3
  56.5 1.1 copy-start.16
  57.6 1.0 copy-start.11
  58.6 2.9 copy-start.7
  64.6 0.8 slice-start.1
  65.4 23.9 %copy-start.20 = (f32[256]{0:T(256)S(1)}, f32[256]{0:T(256)}, u32[]{:S(2)}) copy-start(f32[256]{0:T(256)} %add_multiply_fusion) | copy-start | bytes 3076
  87.1 2.2 copy-start.12
  87.1 2.5 copy-start.14
  89.6 2.6 slice-start
  89.6 2.6 copy-start.15
  92.2 0.8 copy-start.17
  92.3 0.8 copy-start.21
  93.5 1.7 copy-start.8
  538.5 4.0 copy-start.1
Sparse Core Ops, SparseCore 0:
  15.4 121.9 all-gather.2
  139.0 216.3 all-gather.4
where the time goes:
time: 553 us; the launch traced here: 549 us
  waiting for transfers between devices  223 us (40%)
  other arithmetic  177 us (32%)
  local copies, waits for them, and re-layouts  107 us (19%)
  blocking collectives  21.6 us (4%)
  between operations  13.8 us (2%)
    all_gather x1, waiting for transfers between devices, per_device(): lax.all_gather(forced, 'gz', axis=1, tiled=True)  181 us
    while x96, other arithmetic  119 us
    all_gather x1, waiting for transfers between devices, per_device(): lax.all_gather(coupling, 'gz', axis=1, tiled=True)  42.2 us
    dynamic_update_slice x24, local copies, waits for them, and re-layouts, thomas(): lax.scan(forward, (ratio_start, zero_level), (rhs_lev, below_lev, above_l...  30.6 us
    concatenate x24, other arithmetic, thomas(): lax.scan(forward, (ratio_start, zero_level), (rhs_lev, below_lev, above_l...  25.3 us
    all_gather x1, blocking collectives, carried_in(): gathered = lax.all_gather(part, axis)  21.6 us
    slice x1, local copies, waits for them, and re-layouts, tridiagonal(): below[:, :-1]  12.7 us
    concatenate x1, local copies, waits for them, and re-layouts, tridiagonal(): jnp.concatenate([jnp.zeros_like(below[:, :1]), below[:, :-1]], axis=1)  11.9 us
  transfers between devices with their start and end apart: 6, of which 2 were waited for; matrix products, arithmetic and copies ran while one was open for 15% of the time, Pallas kernels for 0%

commit v1 on v0

v1 whole, which is shorter than its diff:
```python
import functools

import jax
import jax.numpy as jnp
from jax import lax
from jax.experimental import pallas as pl
from jax.experimental.pallas import tpu as pltpu
from jax.sharding import PartitionSpec as P

MESH = pl.DeviceIdType.MESH
F32 = jnp.float32


def density_of(t, s):
    return t * (-0.3 - 0.05 * t) + 0.7 * s


def as_float(mask):
    return jnp.where(mask, 1.0, 0.0).astype(F32)


def kernel(
    sizes, state, mixing, dep_ref, wind_ref, out,
    st, mx, fr, rat, inv, hx_src, hx, hy_src, hy, south_flux, edge_p,
    s_src, s_in, s_acc, h_src, h_in, h_acc,
    c_out, c_in, mh, h_out, r_in, k_in, k_out, k_a, k_b, d_last,
    st_sem, mx_sem, out_sem, hx_send, hx_recv, hy_send, hy_recv,
    s_send, s_recv, h_send, h_recv, c_send, c_recv, m_send, m_recv, r_send, r_recv, x_send,
):
    gx_n, gy_n, gz_n = sizes
    _, levels, cols, rows = st.shape
    total_x, total_y = dep_ref.shape
    blocks = rows // 128
    half = gz_n // 2
    ix, iy, z = lax.axis_index("gx"), lax.axis_index("gy"), lax.axis_index("gz")
    east, west = lax.rem(ix + 1, gx_n), lax.rem(ix + gx_n - 1, gx_n)
    has_north, has_south = iy < gy_n - 1, iy > 0
    down = z < half
    step = jnp.where(down, 1, -1)
    first = jnp.where(down, 0, levels - 1)
    final = jnp.where(down, levels - 1, 0)
    has_out = (z > 0) & (z < gz_n - 1)
    mid = (z == half - 1) | (z == half)
    base = z * levels

    loads = [pltpu.make_async_copy(state.at[f], st.at[f], st_sem.at[f]) for f in range(4)]
    for copy in loads:
        copy.start()
    load_mx = pltpu.make_async_copy(mixing, mx, mx_sem)
    load_mx.start()

    barrier = pltpu.get_barrier_semaphore()
    for other in (east, west):
        pl.semaphore_signal(barrier, inc=1, device_id={"gx": other}, device_id_type=MESH)
    for d in range(1, gz_n):
        pl.semaphore_signal(barrier, inc=1, device_id={"gz": lax.rem(z + d, gz_n)}, device_id_type=MESH)

    @pl.when(has_north)
    def _():
        pl.semaphore_signal(barrier, inc=1, device_id={"gy": iy + 1}, device_id_type=MESH)

    @pl.when(has_south)
    def _():
        pl.semaphore_signal(barrier, inc=1, device_id={"gy": iy - 1}, device_id_type=MESH)

    greeted = 2 + (gz_n - 1) + jnp.where(has_north, 1, 0) + jnp.where(has_south, 1, 0)
    pl.semaphore_wait(barrier, greeted)

    def remote(src, dst, send, recv, **device):
        return pltpu.make_async_remote_copy(
            src_ref=src, dst_ref=dst, send_sem=send, recv_sem=recv, device_id=device, device_id_type=MESH
        )

    def mixing_copy(target):
        return remote(mixing.at[:, levels - 1], mh, m_send, m_recv, gz=target)

    sends_mixing = (z >= half) & (z < gz_n - 1)

    @pl.when(sends_mixing)
    def _():
        mixing_copy(z + 1).start()

    lane = lax.broadcasted_iota(jnp.int32, (cols, 128), 1)
    lane_wide = lax.broadcasted_iota(jnp.int32, (cols, rows), 1)
    row_wide = lax.broadcasted_iota(jnp.int32, (cols, rows), 0)

    for copy in loads:
        copy.wait()

    def rows_out(k, carry):
        for f in range(4):
            hx_src[0, f, pl.ds(k, 1), :] = st[f, k, cols - 1:cols, :]
            hx_src[1, f, pl.ds(k, 1), :] = st[f, k, 0:1, :]
        return carry

    lax.fori_loop(0, levels, rows_out, 0)
    x_copies = [
        remote(hx_src.at[0], hx.at[0], hx_send.at[0], hx_recv.at[0], gx=east),
        remote(hx_src.at[1], hx.at[1], hx_send.at[1], hx_recv.at[1], gx=west),
    ]
    for copy in x_copies:
        copy.start()

    y_copies = [
        remote(hy_src.at[0], hy.at[0], hy_send.at[0], hy_recv.at[0], gy=lax.rem(iy + 1, gy_n)),
        remote(hy_src.at[1], hy.at[1], hy_send.at[1], hy_recv.at[1], gy=lax.rem(iy + gy_n - 1, gy_n)),
    ]
    zero = jnp.zeros((cols, 128), F32)

    def pack(side):
        def one(k, packed):
            shift = k + 1 if side == 0 else k
            lanes = pl.ds(rows - 128, 128) if side == 0 else pl.ds(0, 128)
            return tuple(
                jnp.where(lane == k, pltpu.roll(st[f, k, :, lanes], shift, 1), packed[f]) for f in range(4)
            )

        packed = lax.fori_loop(0, levels, one, (zero,) * 4)
        for f in range(4):
            hy_src[side, f] = packed[f]

    for side, present, absent_in in ((0, has_north, 1), (1, has_south, 0)):

        @pl.when(present)
        def _(side=side):
            pack(side)
            y_copies[side].start()

        @pl.when(jnp.logical_not(present))
        def _(side=side, absent_in=absent_in):
            for f in range(4):
                hy_src[side, f] = zero
                hy[absent_in, f] = zero

    start_x = pl.multiple_of(ix * cols, cols)
    start_y = pl.multiple_of(iy * rows, rows)
    dep = dep_ref[pl.ds(start_x, cols), pl.ds(start_y, rows)]
    dep_w = dep_ref[pl.ds(lax.rem(start_x + total_x - 1, total_x), 1), pl.ds(start_y, rows)]
    dep_e = dep_ref[pl.ds(lax.rem(start_x + cols, total_x), 1), pl.ds(start_y, rows)]
    block_s = pl.multiple_of(lax.rem(start_y + total_y - 128, total_y), 128)
    block_n = pl.multiple_of(lax.rem(start_y + rows, total_y), 128)
    dep_s = dep_ref[pl.ds(start_x, cols), pl.ds(block_s, 128)][:, 127:128]
    dep_n = dep_ref[pl.ds(start_x, cols), pl.ds(block_n, 128)][:, 0:1]
    dep_s = jnp.where(has_south, dep_s, 0)
    dep_n = jnp.where(has_north, dep_n, 0)

    def from_east(array, row):
        return jnp.where(row_wide == cols - 1, row, pltpu.roll(array, cols - 1, 0))

    def from_west(array, row):
        return jnp.where(row_wide == 0, row, pltpu.roll(array, 1, 0))

    def from_north(array, block):
        wide = jnp.concatenate([block] * blocks, axis=1)
        return jnp.where(lane_wide == rows - 1, wide, pltpu.roll(array, rows - 1, 1))

    def from_south(array, block):
        wide = jnp.concatenate([block] * blocks, axis=1)
        return jnp.where(lane_wide == 0, wide, pltpu.roll(array, 1, 1))

    least_e = jnp.minimum(dep, from_east(dep, dep_e))
    least_n = jnp.minimum(dep, from_north(dep, jnp.broadcast_to(dep_n, (cols, 128))))
    least_w = jnp.minimum(dep[0:1], dep_w)

    def total_one(k, total):
        return total + density_of(st[0, k], st[1, k]) * as_float(base + k < dep)

    s_src[...] = lax.fori_loop(0, levels, total_one, jnp.zeros((cols, rows), F32))

    def s_copy(d, slot):
        return remote(s_src, s_in.at[slot], s_send.at[d - 1], s_recv.at[slot], gz=lax.rem(z + d, gz_n))

    def h_copy(d, slot):
        return remote(h_src, h_in.at[slot], h_send.at[d - 1], h_recv.at[slot], gz=lax.rem(z + d, gz_n))

    for d in range(1, gz_n):

        @pl.when(z + d < gz_n)
        def _(d=d):
            s_copy(d, z).start()

    load_mx.wait()
    slot_in = jnp.where(mid, 1, 0)
    inward = jnp.clip(z + step, 0, gz_n - 1)
    outward = jnp.clip(z - step, 0, gz_n - 1)
    other_z = lax.rem(z + 1, gz_n)

    def below(m):
        return mx[m, levels - 1] * as_float(base + levels < dep)

    for m in range(2):
        d_last[m] = jnp.ones((cols, rows), F32)

    @pl.when(has_out)
    def _():
        remote(c_out, c_in.at[0], c_send, c_recv.at[0], gz=other_z).wait_recv()
        for m in range(2):
            into = c_in[0, m]

            @pl.when(down)
            def _(m=m, into=into):
                k_in[m] = jnp.ones((cols, rows), F32)
                d_last[m] = 1.0 + into

            @pl.when(jnp.logical_not(down))
            def _(m=m, into=into):
                c = below(m)
                ratio = c / (into + c)
                k_in[m] = ratio
                d_last[m] = 1.0 + ratio * into

    def coefficient(t, ds):
        k = first + step * t
        ci = jnp.where(down, k, k - 1)
        wet = as_float(base + ci + 1 < dep)
        new = []
        for m in range(2):
            c = mx[m, ci] * wet
            over = 1.0 / (ds[m] + c)
            ratio = c * over
            rat[m, k] = ratio
            inv[m, k] = over
            new.append(1.0 + ratio * ds[m])
        return tuple(new)

    ds = lax.fori_loop(0, levels - 1, coefficient, (d_last[0], d_last[1]))
    for m in range(2):
        d_last[m] = ds[m]

    @pl.when(down)
    def _():
        for m in range(2):
            c = below(m)
            ratio = c / (d_last[m] + c)
            k_out[m] = ratio
            c_out[m] = ratio * d_last[m]

    @pl.when(jnp.logical_not(down))
    def _():
        for m in range(2):
            k_out[m] = jnp.ones((cols, rows), F32)
            c_out[m] = d_last[m]

    c_copy = remote(c_out, c_in.at[slot_in], c_send, c_recv.at[slot_in], gz=inward)
    c_copy.start()

    for copy in x_copies:
        copy.wait_recv()

    @pl.when(has_south)
    def _():
        y_copies[0].wait_recv()

    @pl.when(has_north)
    def _():
        y_copies[1].wait_recv()

    def total_rows(k, totals):
        at = pl.ds(k, 1)
        w = density_of(hx[0, 0, at, :], hx[0, 1, at, :]) * as_float(base + k < dep_w)
        e = density_of(hx[1, 0, at, :], hx[1, 1, at, :]) * as_float(base + k < dep_e)
        return totals[0] + w, totals[1] + e

    row_zero = jnp.zeros((1, rows), F32)
    tot_w, tot_e = lax.fori_loop(0, levels, total_rows, (row_zero, row_zero))

    lane_level = jnp.where(lane < levels, base + lane, 1 << 20)

    def running(dens):
        sh = 1
        while sh < levels:
            dens = dens + jnp.where(lane >= sh, pltpu.roll(dens, sh, 1), 0.0)
            sh *= 2
        return dens

    dens_n = density_of(hy[1, 0], hy[1, 1]) * as_float(lane_level < dep_n)
    dens_s = density_of(hy[0, 0], hy[0, 1]) * as_float(lane_level < dep_s)
    dens_o = density_of(hy_src[1, 0], hy_src[1, 1]) * as_float(lane_level < dep[:, 0:1])
    tot_n = jnp.sum(dens_n, axis=1, keepdims=True)
    tot_s = jnp.sum(dens_s, axis=1, keepdims=True)
    h_src[0:cols, :] = jnp.where(lane == 0, tot_s, jnp.where(lane == 1, tot_n, 0.0))
    for b in range(blocks):
        part = slice(b * 128, b * 128 + 128)
        at = cols + 8 * b
        h_src[at:at + 8, :] = jnp.concatenate([tot_w[:, part], tot_e[:, part], jnp.zeros((6, 128), F32)], axis=0)

    for d in range(1, gz_n):

        @pl.when(z + d < gz_n)
        def _(d=d):
            h_copy(d, z).start()

    s_acc[...] = jnp.zeros_like(s_acc)
    h_acc[...] = jnp.zeros_like(h_acc)
    for p in range(gz_n - 1):

        @pl.when(z > p)
        def _(p=p):
            s_copy(1, p).wait_recv()
            s_acc[...] = s_acc[...] + s_in[p]
            h_copy(1, p).wait_recv()
            h_acc[...] = h_acc[...] + h_in[p]

    edge_p[0] = h_acc[0:cols, 1:2] + running(dens_n) - 0.5 * dens_n
    p_s = h_acc[0:cols, 0:1] + running(dens_s) - 0.5 * dens_s
    p_o = s_acc[:, 0:1] + running(dens_o) - 0.5 * dens_o
    mask_s = as_float(lane_level < jnp.minimum(dep_s, dep[:, 0:1]))
    edge_p[1] = mask_s * (p_o - p_s)
    vel = 0.5 * (hy[0, 3] + hy_src[1, 3]) * mask_s
    take_s = 0.25 * jnp.maximum(vel, 0.0) + 0.08 * mask_s
    take_n = 0.25 * jnp.minimum(vel, 0.0) - 0.08 * mask_s
    for f in range(4):
        south_flux[f] = take_s * hy[0, f] + take_n * hy_src[1, f]

    sign = jnp.where(down, 1.0, -1.0).astype(F32)
    own = jnp.where(down, 0.0, 1.0).astype(F32)

    def wide_row(ref, r):
        return jnp.concatenate([ref[cols + 8 * b + r:cols + 8 * b + r + 1, :] for b in range(blocks)], axis=1)

    run = s_acc[...] + own * s_src[...]
    run_w = wide_row(h_acc, 0) + own * wide_row(h_src, 0)
    run_e = wide_row(h_acc, 1) + own * wide_row(h_src, 1)
    coriolis = 0.3 * (0.5 + ((start_y + lane_wide).astype(F32) + 0.5) / total_y)

    def advance(t, carry):
        run, run_w, run_e = carry
        k = first + step * t
        kg = base + k
        at = pl.ds(k, 1)
        c = [st[f, k] for f in range(4)]
        w = [hx[0, f, at, :] for f in range(4)]
        e = [hx[1, f, at, :] for f in range(4)]
        to_north = 127 - k
        to_south = lax.rem(128 - k, 128)
        wet = as_float(kg < dep)
        mask_x = as_float(kg < least_e)
        mask_y = as_float(kg < least_n)
        mask_w = as_float(kg < least_w)
        c_e = [from_east(c[f], e[f]) for f in range(4)]
        c_n = [from_north(c[f], pltpu.roll(hy[1, f], to_north, 1)) for f in range(4)]

        def takes(vel, mask):
            return 0.25 * jnp.maximum(vel, 0.0) + 0.08 * mask, 0.25 * jnp.minimum(vel, 0.0) - 0.08 * mask

        ax, bx = takes(0.5 * (c[2] + c_e[2]) * mask_x, mask_x)
        aw, bw = takes(0.5 * (w[2] + c[2][0:1]) * mask_w, mask_w)
        ay, by = takes(0.5 * (c[3] + c_n[3]) * mask_y, mask_y)
        moved = []
        for f in range(4):
            flux_x = ax * c[f] + bx * c_e[f]
            flux_y = ay * c[f] + by * c_n[f]
            flux_w = from_west(flux_x, aw * w[f] + bw * c[f][0:1])
            flux_s = from_south(flux_y, pltpu.roll(south_flux[f], to_south, 1))
            moved.append(c[f] - (flux_x - flux_w + flux_y - flux_s))

        dens = density_of(c[0], c[1]) * wet
        dens_w = density_of(w[0], w[1]) * as_float(kg < dep_w)
        dens_e = density_of(e[0], e[1]) * as_float(kg < dep_e)
        p = run + (0.5 * sign) * dens
        p_w = run_w + (0.5 * sign) * dens_w
        p_e = run_e + (0.5 * sign) * dens_e
        g_x = mask_x * (from_east(p, p_e) - p)
        g_y = mask_y * (from_north(p, pltpu.roll(edge_p[0], to_north, 1)) - p)
        g_x = g_x + from_west(g_x, mask_w * (p[0:1] - p_w))
        g_y = g_y + from_south(g_y, pltpu.roll(edge_p[1], to_south, 1))
        top = jnp.where(kg == 0, 1.0, 0.0).astype(F32)
        fr[0, k] = moved[0] * wet
        fr[1, k] = moved[1] * wet
        fr[2, k] = (moved[2] + coriolis * c[3] - 0.015 * g_x + top * wind_ref[0]) * wet
        fr[3, k] = (moved[3] - coriolis * c[2] - 0.015 * g_y + top * wind_ref[1]) * wet
        return run + sign * dens, run_w + sign * dens_w, run_e + sign * dens_e

    lax.fori_loop(0, levels, advance, (run, run_w, run_e))

    @pl.when(mid)
    def _():
        remote(c_out, c_in.at[1], c_send, c_recv.at[1], gz=other_z).wait_recv()

    receives_mixing = z > half

    @pl.when(receives_mixing)
    def _():
        mixing_copy(other_z).wait_recv()

    for m in range(2):

        @pl.when(down & jnp.logical_not(mid))
        def _(m=m):
            c = below(m)
            over = 1.0 / (d_last[m] + c)
            k_a[m] = over
            k_b[m] = c * over

        @pl.when(receives_mixing)
        def _(m=m):
            c = mh[m] * as_float(base < dep)
            over = 1.0 / (d_last[m] + c)
            k_a[m] = over
            k_b[m] = c * over

        @pl.when(z == half - 1)
        def _(m=m):
            c = below(m)
            ratio = c / (c_in[1, m] + c)
            over = 1.0 / (d_last[m] + ratio * c_in[1, m])
            k_a[m] = over
            k_b[m] = ratio * over

        @pl.when(z == half)
        def _(m=m):
            over = 1.0 / (d_last[m] + c_in[1, m])
            k_a[m] = over
            k_b[m] = over

    in_copies = [remote(h_out.at[f], r_in.at[slot_in, f], r_send.at[f], r_recv.at[slot_in, f], gz=inward) for f in range(4)]
    out_copies = [remote(fr.at[f, first], r_in.at[1, f], x_send.at[f], r_recv.at[1, f], gz=outward) for f in range(4)]
    stores = [pltpu.make_async_copy(fr.at[f], out.at[f], out_sem.at[f]) for f in range(4)]

    for f in range(4):
        m = f // 2

        @pl.when(has_out)
        def _(f=f, m=m):
            remote(h_out.at[f], r_in.at[0, f], r_send.at[f], r_recv.at[0, f], gz=other_z).wait_recv()
            fr[f, first] = fr[f, first] + k_in[m] * r_in[0, f]

        def forward(t, g, f=f, m=m):
            k = first + step * t
            g = fr[f, k] + rat[m, k - step] * g
            fr[f, k] = g
            return g

        g = lax.fori_loop(1, levels, forward, fr[f, first])
        h_out[f] = k_out[m] * g
        in_copies[f].start()

    for f in range(4):
        m = f // 2
        remote(h_out.at[f], r_in.at[1, f], r_send.at[f], r_recv.at[1, f], gz=other_z).wait_recv()
        x = k_a[m] * fr[f, final] + k_b[m] * r_in[1, f]
        fr[f, final] = x

        def backward(t, x, f=f, m=m):
            k = final - step * t
            x = inv[m, k] * fr[f, k] + rat[m, k] * x
            fr[f, k] = x
            return x

        lax.fori_loop(1, levels, backward, x)

        @pl.when(has_out)
        def _(f=f):
            out_copies[f].start()

        stores[f].start()

    for copy in x_copies:
        copy.wait_send()
    for side, present in ((0, has_north), (1, has_south)):

        @pl.when(present)
        def _(side=side):
            y_copies[side].wait_send()

    for d in range(1, gz_n):

        @pl.when(z + d < gz_n)
        def _(d=d):
            s_copy(d, z).wait_send()
            h_copy(d, z).wait_send()

    @pl.when(sends_mixing)
    def _():
        mixing_copy(z + 1).wait_send()

    c_copy.wait_send()
    for f in range(4):
        in_copies[f].wait_send()

        @pl.when(has_out)
        def _(f=f):
            out_copies[f].wait_send()

        stores[f].wait()


def per_device(sizes, state, mixing, depth_levels, wind):
    _, levels, cols, rows = state.shape
    gz_n = sizes[2]
    blocks = rows // 128
    any_spec = pl.BlockSpec(memory_space=pl.ANY)
    vmem_spec = pl.BlockSpec(memory_space=pltpu.VMEM)
    vmem = lambda *shape: pltpu.VMEM(shape, F32)
    dma = lambda *shape: pltpu.SemaphoreType.DMA(shape)
    tile = (cols, rows)
    earlier = max(gz_n - 1, 1)
    h_rows = cols + 8 * blocks
    one = pltpu.SemaphoreType.DMA
    scratch = [
        vmem(4, levels, *tile), vmem(2, levels, *tile), vmem(4, levels, *tile),
        vmem(2, levels, *tile), vmem(2, levels, *tile),
        vmem(2, 4, levels, rows), vmem(2, 4, levels, rows), vmem(2, 4, cols, 128), vmem(2, 4, cols, 128),
        vmem(4, cols, 128), vmem(2, cols, 128),
        vmem(*tile), vmem(earlier, *tile), vmem(*tile),
        vmem(h_rows, 128), vmem(earlier, h_rows, 128), vmem(h_rows, 128),
        vmem(2, *tile), vmem(2, 2, *tile), vmem(2, *tile), vmem(4, *tile), vmem(2, 4, *tile),
        vmem(2, *tile), vmem(2, *tile), vmem(2, *tile), vmem(2, *tile), vmem(2, *tile),
        dma(4), one, dma(4), dma(2), dma(2), dma(2), dma(2),
        dma(earlier), dma(earlier), dma(earlier), dma(earlier), one, dma(2), one, one, dma(4), dma(2, 4), dma(4),
    ]
    return pl.pallas_call(
        functools.partial(kernel, sizes),
        out_shape=jax.ShapeDtypeStruct(state.shape, F32),
        in_specs=[any_spec, any_spec, vmem_spec, vmem_spec],
        out_specs=any_spec,
        scratch_shapes=scratch,
        compiler_params=pltpu.CompilerParams(
            collective_id=0, has_side_effects=True, vmem_limit_bytes=40 * 1024 * 1024
        ),
        cost_estimate=pl.CostEstimate(flops=state.size * 60, bytes_accessed=state.size * 10, transcendentals=0),
    )(state, mixing, depth_levels, wind)


def solution(mesh):
    sizes = tuple(mesh.shape[name] for name in ("gx", "gy", "gz"))
    return jax.shard_map(
        functools.partial(per_device, sizes),
        mesh=mesh,
        in_specs=(P(None, "gz", "gx", "gy"), P(None, "gz", "gx", "gy"), P(), P(None, "gx", "gy")),
        out_specs=P(None, "gz", "gx", "gy"),
        check_vma=False,
    )
```

time: 553 us -> 43.8 us (0.08)
  waiting for transfers between devices: 223 us -> 0 us
  other arithmetic: 177 us -> 0 us
  local copies, waits for them, and re-layouts: 107 us -> 6.75 us
  Pallas kernels: 0 us -> 36.8 us
  blocking collectives: 21.6 us -> 0 us
  between operations: 13.8 us -> 0.01 us
    all_gather x2 -> x0, waiting for transfers between devices: 223 us -> none  [the longest x1 181 us: per_device(): lax.all_gather(forced, 'gz', axis=1, tiled=True)]
    while x96 -> x0, other arithmetic: 119 us -> none
    pallas_call x0 -> x1, Pallas kernels: none -> 36.8 us  [per_device(): pl.pallas_call(functools.partial(kernel, sizes), out_shape=jax.ShapeDtype...]
    dynamic_update_slice x24 -> x0, local copies, waits for them, and re-layouts: 30.6 us -> none  [thomas(): lax.scan(forward, (ratio_start, zero_level), (rhs_lev, below_lev, above_l...]
    concatenate x25 -> x0, other arithmetic: 26 us -> none  [the longest x24 25.3 us: thomas(): lax.scan(forward, (ratio_start, zero_level), (rhs_lev, below_lev, above_l...]
    slice x11 -> x0, local copies, waits for them, and re-layouts: 22 us -> none  [the longest x1 12.7 us: tridiagonal(): below[:, :-1]]
    all_gather x1 -> x0, blocking collectives: 21.6 us -> none  [carried_in(): gathered = lax.all_gather(part, axis)]
    concatenate x14 -> x0, local copies, waits for them, and re-layouts: 14.9 us -> none  [the longest x1 11.9 us: tridiagonal(): jnp.concatenate([jnp.zeros_like(below[:, :1]), below[:, :-1]], axis=1)]
  transfers between devices with their start and end apart: 6 -> 0, of which waited for: 2 -> 0; matrix products, arithmetic and copies ran while one was open for 15% -> 0% of each run, Pallas kernels for 0% -> 0%
where the time goes in v1:
time: 43.8 us; the launch traced here: 43.5 us
  Pallas kernels  36.8 us (84%)
  local copies, waits for them, and re-layouts  6.75 us (15%)
    pallas_call x1, Pallas kernels, per_device(): pl.pallas_call(functools.partial(kernel, sizes), out_shape=jax.ShapeDtype...  36.8 us
    unnamed x9, local copies, waits for them, and re-layouts  6.75 us

profile of v1, /device:TPU:0, one launch (start us, length us, event | category | flops | bytes accessed | tf_op | source)
XLA Modules:
  0.0 43.5 jit_solution(6160188401799398902)
XLA Ops:
  0.0 0.0 copy-start
  0.0 1.9 %copy-done = f32[4,24,32,256]{3,2,1,0:T(8,128)S(1)} copy-done((f32[4,24,32,256]{3,2,1,0:T(8,128)S(1)}, f32[4,24,32,256]{3,2,1,0:T(8,128)}, u32[]{:S(2)}) %copy-start) | copy-done | bytes 3145752
  1.9 0.0 copy-start.1
  1.9 1.4 %copy-done.1 = f32[2,24,32,256]{3,2,1,0:T(8,128)S(1)} copy-done((f32[2,24,32,256]{3,2,1,0:T(8,128)S(1)}, f32[2,24,32,256]{3,2,1,0:T(8,128)}, u32[]{:S(2)}) %copy-start.1) | copy-done | bytes 1572888
  3.3 0.0 copy-start.2
  3.3 0.9 %copy-done.2 = s32[128,512]{1,0:T(8,128)S(1)} copy-done((s32[128,512]{1,0:T(8,128)S(1)}, s32[128,512]{1,0:T(8,128)}, u32[]{:S(2)}) %copy-start.2) | copy-done | bytes 262168
  4.2 0.0 copy-start.3
  4.3 0.8 %copy-done.3 = f32[2,32,256]{2,1,0:T(8,128)S(1)} copy-done((f32[2,32,256]{2,1,0:T(8,128)S(1)}, f32[2,32,256]{2,1,0:T(8,128)}, u32[]{:S(2)}) %copy-start.3) | copy-done | bytes 65560
  5.1 36.8 %shard_map.46 = f32[4,24,32,256]{3,2,1,0:T(8,128)S(1)} custom-call(f32[4,24,32,256]{3,2,1,0:T(8,128)S(1)} %copy-done, f32[2,24,32,256]{3,2,1,0:T(8,128)S(1)} %copy-done.1, s32[128,512]{1,0:T(8,128)S(1)} %copy-done.2, f32[2,32,256]{2,1,0:T(8,128)S(1)} %copy-done.3), custom_call_target="tpu_custom_call" | custom-call | flops 47185920 | bytes 7864320 | tf_op jit(solution)/shard_map/pallas_call | solution.py:512
  41.9 1.7 %copy.6 = f32[4,24,32,256]{3,2,1,0:T(8,128)} copy(f32[4,24,32,256]{3,2,1,0:T(8,128)S(1)} %shard_map.46) | data formatting | bytes 6291456
Async XLA Ops:
  0.0 1.9 %copy-start = (f32[4,24,32,256]{3,2,1,0:T(8,128)S(1)}, f32[4,24,32,256]{3,2,1,0:T(8,128)}, u32[]{:S(2)}) copy-start(f32[4,24,32,256]{3,2,1,0:T(8,128)} %state.1) | copy-start | bytes 9437188
  1.9 1.4 %copy-start.1 = (f32[2,24,32,256]{3,2,1,0:T(8,128)S(1)}, f32[2,24,32,256]{3,2,1,0:T(8,128)}, u32[]{:S(2)}) copy-start(f32[2,24,32,256]{3,2,1,0:T(8,128)} %mixing.1) | copy-start | bytes 4718596
  3.3 0.9 %copy-start.2 = (s32[128,512]{1,0:T(8,128)S(1)}, s32[128,512]{1,0:T(8,128)}, u32[]{:S(2)}) copy-start(s32[128,512]{1,0:T(8,128)} %dep_ref.1) | copy-start | bytes 786436
  4.2 0.8 %copy-start.3 = (f32[2,32,256]{2,1,0:T(8,128)S(1)}, f32[2,32,256]{2,1,0:T(8,128)}, u32[]{:S(2)}) copy-start(f32[2,32,256]{2,1,0:T(8,128)} %wind_ref.1) | copy-start | bytes 196612

commit v2 on v1

--- a/solution.py
+++ b/solution.py
@@ -20,16 +20,16 @@
 
 
 def kernel(
-    sizes, state, mixing, dep_ref, wind_ref, out,
-    st, mx, fr, rat, inv, hx_src, hx, hy_src, hy, south_flux, edge_p,
+    sizes, state, mixing, dep_any, wind_any, out,
+    dep_ref, wind_ref, st, mx, fr, rat, inv, take, take_w, via, w_last, hx_src, hx, hy_src, hy, south_flux, edge_p,
     s_src, s_in, s_acc, h_src, h_in, h_acc,
     c_out, c_in, mh, h_out, r_in, k_in, k_out, k_a, k_b, d_last,
-    st_sem, mx_sem, out_sem, hx_send, hx_recv, hy_send, hy_recv,
+    dep_sem, wind_sem, st_sem, mx_sem, out_sem, hx_send, hx_recv, hy_send, hy_recv,
     s_send, s_recv, h_send, h_recv, c_send, c_recv, m_send, m_recv, r_send, r_recv, x_send,
 ):
     gx_n, gy_n, gz_n = sizes
     _, levels, cols, rows = st.shape
-    total_x, total_y = dep_ref.shape
+    total_x, total_y = dep_any.shape
     blocks = rows // 128
     half = gz_n // 2
     ix, iy, z = lax.axis_index("gx"), lax.axis_index("gy"), lax.axis_index("gz")
@@ -46,8 +46,12 @@
     loads = [pltpu.make_async_copy(state.at[f], st.at[f], st_sem.at[f]) for f in range(4)]
     for copy in loads:
         copy.start()
+    load_dep = pltpu.make_async_copy(dep_any, dep_ref, dep_sem)
+    load_dep.start()
     load_mx = pltpu.make_async_copy(mixing, mx, mx_sem)
     load_mx.start()
+    load_wind = pltpu.make_async_copy(wind_any, wind_ref, wind_sem)
+    load_wind.start()
 
     barrier = pltpu.get_barrier_semaphore()
     for other in (east, west):
@@ -82,7 +86,6 @@
 
     lane = lax.broadcasted_iota(jnp.int32, (cols, 128), 1)
     lane_wide = lax.broadcasted_iota(jnp.int32, (cols, rows), 1)
-    row_wide = lax.broadcasted_iota(jnp.int32, (cols, rows), 0)
 
     for copy in loads:
         copy.wait()
@@ -132,6 +135,7 @@
                 hy_src[side, f] = zero
                 hy[absent_in, f] = zero
 
+    load_dep.wait()
     start_x = pl.multiple_of(ix * cols, cols)
     start_y = pl.multiple_of(iy * rows, rows)
     dep = dep_ref[pl.ds(start_x, cols), pl.ds(start_y, rows)]
@@ -144,19 +148,24 @@
     dep_s = jnp.where(has_south, dep_s, 0)
     dep_n = jnp.where(has_north, dep_n, 0)
 
+    tile_row = lax.broadcasted_iota(jnp.int32, (8, rows), 0)
+    tiles = cols // 8
+
     def from_east(array, row):
-        return jnp.where(row_wide == cols - 1, row, pltpu.roll(array, cols - 1, 0))
+        turned = [pltpu.roll(array[8 * i:8 * i + 8], 7, 0) for i in range(tiles)] + [row]
+        return jnp.concatenate([jnp.where(tile_row == 7, turned[i + 1], turned[i]) for i in range(tiles)], axis=0)
 
     def from_west(array, row):
-        return jnp.where(row_wide == 0, row, pltpu.roll(array, 1, 0))
+        turned = [row] + [pltpu.roll(array[8 * i:8 * i + 8], 1, 0) for i in range(tiles)]
+        return jnp.concatenate([jnp.where(tile_row == 0, turned[i], turned[i + 1]) for i in range(tiles)], axis=0)
 
     def from_north(array, block):
-        wide = jnp.concatenate([block] * blocks, axis=1)
-        return jnp.where(lane_wide == rows - 1, wide, pltpu.roll(array, rows - 1, 1))
+        turned = [pltpu.roll(array[:, 128 * b:128 * b + 128], 127, 1) for b in range(blocks)] + [block]
+        return jnp.concatenate([jnp.where(lane == 127, turned[b + 1], turned[b]) for b in range(blocks)], axis=1)
 
     def from_south(array, block):
-        wide = jnp.concatenate([block] * blocks, axis=1)
-        return jnp.where(lane_wide == 0, wide, pltpu.roll(array, 1, 1))
+        turned = [block] + [pltpu.roll(array[:, 128 * b:128 * b + 128], 1, 1) for b in range(blocks)]
+        return jnp.concatenate([jnp.where(lane == 0, turned[b], turned[b + 1]) for b in range(blocks)], axis=1)
 
     least_e = jnp.minimum(dep, from_east(dep, dep_e))
     least_n = jnp.minimum(dep, from_north(dep, jnp.broadcast_to(dep_n, (cols, 128))))
@@ -184,65 +193,57 @@
     inward = jnp.clip(z + step, 0, gz_n - 1)
     outward = jnp.clip(z - step, 0, gz_n - 1)
     other_z = lax.rem(z + 1, gz_n)
+    c_copy = remote(c_out, c_in.at[slot_in], c_send, c_recv.at[slot_in], gz=inward)
 
     def below(m):
         return mx[m, levels - 1] * as_float(base + levels < dep)
 
-    for m in range(2):
-        d_last[m] = jnp.ones((cols, rows), F32)
-
-    @pl.when(has_out)
-    def _():
-        remote(c_out, c_in.at[0], c_send, c_recv.at[0], gz=other_z).wait_recv()
+    def coefficients():
+        def coefficient(t, carry):
+            k = first + step * t
+            ci = jnp.where(down, k, k - 1)
+            wet = as_float(base + ci + 1 < dep)
+            new = []
+            for m in range(2):
+                c = mx[m, ci] * wet
+                over = 1.0 / (carry[m] + c)
+                ratio = c * over
+                rat[m, k + step] = ratio
+                inv[m, k] = over
+                new.append(1.0 + ratio * carry[m])
+            via[k] = over * carry[2]
+            new.append(ratio * carry[2])
+            return tuple(new)
+
+        carry = lax.fori_loop(0, levels - 1, coefficient, (d_last[0], d_last[1], w_last[...]))
         for m in range(2):
-            into = c_in[0, m]
-
-            @pl.when(down)
-            def _(m=m, into=into):
-                k_in[m] = jnp.ones((cols, rows), F32)
-                d_last[m] = 1.0 + into
-
-            @pl.when(jnp.logical_not(down))
-            def _(m=m, into=into):
+            d_last[m] = carry[m]
+            rat[m, first] = jnp.zeros((cols, rows), F32)
+        w_last[...] = carry[2]
+
+        @pl.when(down)
+        def _():
+            for m in range(2):
                 c = below(m)
-                ratio = c / (into + c)
-                k_in[m] = ratio
-                d_last[m] = 1.0 + ratio * into
-
-    def coefficient(t, ds):
-        k = first + step * t
-        ci = jnp.where(down, k, k - 1)
-        wet = as_float(base + ci + 1 < dep)
-        new = []
+                ratio = c / (d_last[m] + c)
+                k_out[m] = ratio
+                c_out[m] = ratio * d_last[m]
+
+        @pl.when(jnp.logical_not(down))
+        def _():
+            for m in range(2):
+                k_out[m] = jnp.ones((cols, rows), F32)
+                c_out[m] = d_last[m]
+
+        c_copy.start()
+
+    @pl.when(jnp.logical_not(has_out))
+    def _():
         for m in range(2):
-            c = mx[m, ci] * wet
-            over = 1.0 / (ds[m] + c)
-            ratio = c * over
-            rat[m, k] = ratio
-            inv[m, k] = over
-            new.append(1.0 + ratio * ds[m])
-        return tuple(new)
-
-    ds = lax.fori_loop(0, levels - 1, coefficient, (d_last[0], d_last[1]))
-    for m in range(2):
-        d_last[m] = ds[m]
-
-    @pl.when(down)
-    def _():
-        for m in range(2):
-            c = below(m)
-            ratio = c / (d_last[m] + c)
-            k_out[m] = ratio
-            c_out[m] = ratio * d_last[m]
-
-    @pl.when(jnp.logical_not(down))
-    def _():
-        for m in range(2):
-            k_out[m] = jnp.ones((cols, rows), F32)
-            c_out[m] = d_last[m]
-
-    c_copy = remote(c_out, c_in.at[slot_in], c_send, c_recv.at[slot_in], gz=inward)
-    c_copy.start()
+            d_last[m] = jnp.ones((cols, rows), F32)
+            r_in[0, 2 + m] = jnp.zeros((cols, rows), F32)
+        w_last[...] = jnp.zeros((cols, rows), F32)
+        coefficients()
 
     for copy in x_copies:
         copy.wait_recv()
@@ -290,6 +291,92 @@
         def _(d=d):
             h_copy(d, z).start()
 
+    mask_s = as_float(lane_level < jnp.minimum(dep_s, dep[:, 0:1]))
+
+    def takes(vel, mask):
+        return 0.25 * jnp.maximum(vel, 0.0) + 0.08 * mask, 0.25 * jnp.minimum(vel, 0.0) - 0.08 * mask
+
+    take_s, take_n = takes(0.5 * (hy[0, 3] + hy_src[1, 3]) * mask_s, mask_s)
+    for f in range(4):
+        south_flux[f] = take_s * hy[0, f] + take_n * hy_src[1, f]
+
+    def moved_of(f, k, c, w, e, c_e, c_n, ax, bx, ay, by, aw, bw):
+        flux_x = ax * c + bx * c_e
+        flux_y = ay * c + by * c_n
+        flux_w = from_west(flux_x, aw * w + bw * c[0:1])
+        flux_s = from_south(flux_y, pltpu.roll(south_flux[f], lax.rem(128 - k, 128), 1))
+        return c - (flux_x - flux_w + flux_y - flux_s)
+
+    def advance_tracers(t, carry):
+        k = first + step * t
+        kg = base + k
+        at = pl.ds(k, 1)
+        to_north = 127 - k
+        mask_x = as_float(kg < least_e)
+        mask_y = as_float(kg < least_n)
+        mask_w = as_float(kg < least_w)
+        u, v = st[2, k], st[3, k]
+        ax, bx = takes(0.5 * (u + from_east(u, hx[1, 2, at, :])) * mask_x, mask_x)
+        ay, by = takes(0.5 * (v + from_north(v, pltpu.roll(hy[1, 3], to_north, 1))) * mask_y, mask_y)
+        aw, bw = takes(0.5 * (hx[0, 2, at, :] + u[0:1]) * mask_w, mask_w)
+        take[0, k], take[1, k], take[2, k], take[3, k] = ax, bx, ay, by
+        take_w[0, at, :], take_w[1, at, :] = aw, bw
+        wet = as_float(kg < dep)
+        for f in range(2):
+            c, w, e = st[f, k], hx[0, f, at, :], hx[1, f, at, :]
+            c_n = from_north(c, pltpu.roll(hy[1, f], to_north, 1))
+            fr[f, k] = moved_of(f, k, c, w, e, from_east(c, e), c_n, ax, bx, ay, by, aw, bw) * wet
+        return carry
+
+    lax.fori_loop(0, levels, advance_tracers, 0)
+
+    @pl.when(has_out)
+    def _():
+        remote(c_out, c_in.at[0], c_send, c_recv.at[0], gz=other_z).wait_recv()
+
+        @pl.when(down)
+        def _():
+            for m in range(2):
+                k_in[m] = jnp.ones((cols, rows), F32)
+                d_last[m] = 1.0 + c_in[0, m]
+
+        @pl.when(jnp.logical_not(down))
+        def _():
+            for m in range(2):
+                c = below(m)
+                ratio = c / (c_in[0, m] + c)
+                k_in[m] = ratio
+                d_last[m] = 1.0 + ratio * c_in[0, m]
+
+        w_last[...] = k_in[1]
+        coefficients()
+
+    in_copies = [remote(h_out.at[f], r_in.at[slot_in, f], r_send.at[f], r_recv.at[slot_in, f], gz=inward) for f in range(4)]
+    out_copies = [remote(fr.at[f, first], r_in.at[1, f], x_send.at[f], r_recv.at[1, f], gz=outward) for f in range(4)]
+    stores = [pltpu.make_async_copy(fr.at[f], out.at[f], out_sem.at[f]) for f in range(4)]
+
+    def wait_in(slot, f):
+        remote(h_out.at[f], r_in.at[slot, f], r_send.at[f], r_recv.at[slot, f], gz=other_z).wait_recv()
+
+    @pl.when(has_out)
+    def _():
+        for f in range(2):
+            wait_in(0, f)
+            fr[f, first] = fr[f, first] + k_in[0] * r_in[0, f]
+
+    def forward(t, g):
+        k = first + step * t
+        ratio = rat[0, k]
+        new = tuple(fr[f, k] + ratio * g[f] for f in range(2))
+        for f in range(2):
+            fr[f, k] = new[f]
+        return new
+
+    g = lax.fori_loop(1, levels, forward, (fr[0, first], fr[1, first]))
+    for f in range(2):
+        h_out[f] = k_out[0] * g[f]
+        in_copies[f].start()
+
     s_acc[...] = jnp.zeros_like(s_acc)
     h_acc[...] = jnp.zeros_like(h_acc)
     for p in range(gz_n - 1):
@@ -304,13 +391,7 @@
     edge_p[0] = h_acc[0:cols, 1:2] + running(dens_n) - 0.5 * dens_n
     p_s = h_acc[0:cols, 0:1] + running(dens_s) - 0.5 * dens_s
     p_o = s_acc[:, 0:1] + running(dens_o) - 0.5 * dens_o
-    mask_s = as_float(lane_level < jnp.minimum(dep_s, dep[:, 0:1]))
     edge_p[1] = mask_s * (p_o - p_s)
-    vel = 0.5 * (hy[0, 3] + hy_src[1, 3]) * mask_s
-    take_s = 0.25 * jnp.maximum(vel, 0.0) + 0.08 * mask_s
-    take_n = 0.25 * jnp.minimum(vel, 0.0) - 0.08 * mask_s
-    for f in range(4):
-        south_flux[f] = take_s * hy[0, f] + take_n * hy_src[1, f]
 
     sign = jnp.where(down, 1.0, -1.0).astype(F32)
     own = jnp.where(down, 0.0, 1.0).astype(F32)
@@ -322,38 +403,27 @@
     run_w = wide_row(h_acc, 0) + own * wide_row(h_src, 0)
     run_e = wide_row(h_acc, 1) + own * wide_row(h_src, 1)
     coriolis = 0.3 * (0.5 + ((start_y + lane_wide).astype(F32) + 0.5) / total_y)
+    load_wind.wait()
 
     def advance(t, carry):
-        run, run_w, run_e = carry
+        run, run_w, run_e, g_u, g_v = carry
         k = first + step * t
         kg = base + k
         at = pl.ds(k, 1)
+        to_north = 127 - k
+        to_south = lax.rem(128 - k, 128)
         c = [st[f, k] for f in range(4)]
         w = [hx[0, f, at, :] for f in range(4)]
         e = [hx[1, f, at, :] for f in range(4)]
-        to_north = 127 - k
-        to_south = lax.rem(128 - k, 128)
         wet = as_float(kg < dep)
         mask_x = as_float(kg < least_e)
         mask_y = as_float(kg < least_n)
         mask_w = as_float(kg < least_w)
-        c_e = [from_east(c[f], e[f]) for f in range(4)]
-        c_n = [from_north(c[f], pltpu.roll(hy[1, f], to_north, 1)) for f in range(4)]
-
-        def takes(vel, mask):
-            return 0.25 * jnp.maximum(vel, 0.0) + 0.08 * mask, 0.25 * jnp.minimum(vel, 0.0) - 0.08 * mask
-
-        ax, bx = takes(0.5 * (c[2] + c_e[2]) * mask_x, mask_x)
-        aw, bw = takes(0.5 * (w[2] + c[2][0:1]) * mask_w, mask_w)
-        ay, by = takes(0.5 * (c[3] + c_n[3]) * mask_y, mask_y)
-        moved = []
-        for f in range(4):
-            flux_x = ax * c[f] + bx * c_e[f]
-            flux_y = ay * c[f] + by * c_n[f]
-            flux_w = from_west(flux_x, aw * w[f] + bw * c[f][0:1])
-            flux_s = from_south(flux_y, pltpu.roll(south_flux[f], to_south, 1))
-            moved.append(c[f] - (flux_x - flux_w + flux_y - flux_s))
-
+        coefs = (take[0, k], take[1, k], take[2, k], take[3, k], take_w[0, at, :], take_w[1, at, :])
+        moved = [None, None]
+        for f in (2, 3):
+            c_n = from_north(c[f], pltpu.roll(hy[1, f], to_north, 1))
+            moved.append(moved_of(f, k, c[f], w[f], e[f], from_east(c[f], e[f]), c_n, *coefs))
         dens = density_of(c[0], c[1]) * wet
         dens_w = density_of(w[0], w[1]) * as_float(kg < dep_w)
         dens_e = density_of(e[0], e[1]) * as_float(kg < dep_e)
@@ -365,13 +435,15 @@
         g_x = g_x + from_west(g_x, mask_w * (p[0:1] - p_w))
         g_y = g_y + from_south(g_y, pltpu.roll(edge_p[1], to_south, 1))
         top = jnp.where(kg == 0, 1.0, 0.0).astype(F32)
-        fr[0, k] = moved[0] * wet
-        fr[1, k] = moved[1] * wet
-        fr[2, k] = (moved[2] + coriolis * c[3] - 0.015 * g_x + top * wind_ref[0]) * wet
-        fr[3, k] = (moved[3] - coriolis * c[2] - 0.015 * g_y + top * wind_ref[1]) * wet
-        return run + sign * dens, run_w + sign * dens_w, run_e + sign * dens_e
-
-    lax.fori_loop(0, levels, advance, (run, run_w, run_e))
+        ratio = rat[1, k]
+        g_u = (moved[2] + coriolis * c[3] - 0.015 * g_x + top * wind_ref[0]) * wet + ratio * g_u
+        g_v = (moved[3] - coriolis * c[2] - 0.015 * g_y + top * wind_ref[1]) * wet + ratio * g_v
+        fr[2, k] = g_u
+        fr[3, k] = g_v
+        return run + sign * dens, run_w + sign * dens_w, run_e + sign * dens_e, g_u, g_v
+
+    wide_zero = jnp.zeros((cols, rows), F32)
+    lax.fori_loop(0, levels, advance, (run, run_w, run_e, wide_zero, wide_zero))
 
     @pl.when(mid)
     def _():
@@ -413,41 +485,57 @@
             k_a[m] = over
             k_b[m] = over
 
-    in_copies = [remote(h_out.at[f], r_in.at[slot_in, f], r_send.at[f], r_recv.at[slot_in, f], gz=inward) for f in range(4)]
-    out_copies = [remote(fr.at[f, first], r_in.at[1, f], x_send.at[f], r_recv.at[1, f], gz=outward) for f in range(4)]
-    stores = [pltpu.make_async_copy(fr.at[f], out.at[f], out_sem.at[f]) for f in range(4)]
-
-    for f in range(4):
-        m = f // 2
-
-        @pl.when(has_out)
-        def _(f=f, m=m):
-            remote(h_out.at[f], r_in.at[0, f], r_send.at[f], r_recv.at[0, f], gz=other_z).wait_recv()
-            fr[f, first] = fr[f, first] + k_in[m] * r_in[0, f]
-
-        def forward(t, g, f=f, m=m):
-            k = first + step * t
-            g = fr[f, k] + rat[m, k - step] * g
-            fr[f, k] = g
-            return g
-
-        g = lax.fori_loop(1, levels, forward, fr[f, first])
-        h_out[f] = k_out[m] * g
+    def backward_tracers():
+        for f in range(2):
+            wait_in(1, f)
+            fr[f, final] = k_a[0] * fr[f, final] + k_b[0] * r_in[1, f]
+
+        def backward(t, x):
+            k = final - step * t
+            ratio, over = rat[0, k + step], inv[0, k]
+            new = tuple(over * fr[f, k] + ratio * x[f] for f in range(2))
+            for f in range(2):
+                fr[f, k] = new[f]
+            return new
+
+        lax.fori_loop(1, levels, backward, (fr[0, final], fr[1, final]))
+        for f in range(2):
+
+            @pl.when(has_out)
+            def _(f=f):
+                out_copies[f].start()
+
+            stores[f].start()
+
+    @pl.when(has_out)
+    def _():
+        backward_tracers()
+        for f in (2, 3):
+            wait_in(0, f)
+            fr[f, final] = fr[f, final] + w_last[...] * r_in[0, f]
+
+    for f in (2, 3):
+        h_out[f] = k_out[1] * fr[f, final]
         in_copies[f].start()
 
-    for f in range(4):
-        m = f // 2
-        remote(h_out.at[f], r_in.at[1, f], r_send.at[f], r_recv.at[1, f], gz=other_z).wait_recv()
-        x = k_a[m] * fr[f, final] + k_b[m] * r_in[1, f]
-        fr[f, final] = x
-
-        def backward(t, x, f=f, m=m):
-            k = final - step * t
-            x = inv[m, k] * fr[f, k] + rat[m, k] * x
-            fr[f, k] = x
-            return x
-
-        lax.fori_loop(1, levels, backward, x)
+    @pl.when(jnp.logical_not(has_out))
+    def _():
+        backward_tracers()
+
+    for f in (2, 3):
+        wait_in(1, f)
+        fr[f, final] = k_a[1] * fr[f, final] + k_b[1] * r_in[1, f]
+
+    def backward(t, x):
+        k = final - step * t
+        ratio, over, add = rat[1, k + step], inv[1, k], via[k]
+        new = tuple(over * fr[2 + i, k] + ratio * x[i] + add * r_in[0, 2 + i] for i in range(2))
+        for i in range(2):
+            fr[2 + i, k] = new[i]
+        return new
+
+    lax.fori_loop(1, levels, backward, (fr[2, final], fr[3, final]))
+    for f in (2, 3):
 
         @pl.when(has_out)
         def _(f=f):
@@ -490,7 +578,6 @@
     gz_n = sizes[2]
     blocks = rows // 128
     any_spec = pl.BlockSpec(memory_space=pl.ANY)
-    vmem_spec = pl.BlockSpec(memory_space=pltpu.VMEM)
     vmem = lambda *shape: pltpu.VMEM(shape, F32)
     dma = lambda *shape: pltpu.SemaphoreType.DMA(shape)
     tile = (cols, rows)
@@ -498,25 +585,27 @@
     h_rows = cols + 8 * blocks
     one = pltpu.SemaphoreType.DMA
     scratch = [
+        pltpu.VMEM(depth_levels.shape, jnp.int32), vmem(2, *tile),
         vmem(4, levels, *tile), vmem(2, levels, *tile), vmem(4, levels, *tile),
         vmem(2, levels, *tile), vmem(2, levels, *tile),
+        vmem(4, levels, *tile), vmem(2, levels, rows), vmem(levels, *tile), vmem(*tile),
         vmem(2, 4, levels, rows), vmem(2, 4, levels, rows), vmem(2, 4, cols, 128), vmem(2, 4, cols, 128),
         vmem(4, cols, 128), vmem(2, cols, 128),
         vmem(*tile), vmem(earlier, *tile), vmem(*tile),
         vmem(h_rows, 128), vmem(earlier, h_rows, 128), vmem(h_rows, 128),
         vmem(2, *tile), vmem(2, 2, *tile), vmem(2, *tile), vmem(4, *tile), vmem(2, 4, *tile),
         vmem(2, *tile), vmem(2, *tile), vmem(2, *tile), vmem(2, *tile), vmem(2, *tile),
-        dma(4), one, dma(4), dma(2), dma(2), dma(2), dma(2),
+        one, one, dma(4), one, dma(4), dma(2), dma(2), dma(2), dma(2),
         dma(earlier), dma(earlier), dma(earlier), dma(earlier), one, dma(2), one, one, dma(4), dma(2, 4), dma(4),
     ]
     return pl.pallas_call(
         functools.partial(kernel, sizes),
         out_shape=jax.ShapeDtypeStruct(state.shape, F32),
-        in_specs=[any_spec, any_spec, vmem_spec, vmem_spec],
+        in_specs=[any_spec] * 4,
         out_specs=any_spec,
         scratch_shapes=scratch,
         compiler_params=pltpu.CompilerParams(
-            collective_id=0, has_side_effects=True, vmem_limit_bytes=40 * 1024 * 1024
+            collective_id=0, has_side_effects=True, vmem_limit_bytes=60 * 1024 * 1024
         ),
         cost_estimate=pl.CostEstimate(flops=state.size * 60, bytes_accessed=state.size * 10, transcendentals=0),
     )(state, mixing, depth_levels, wind)

time: 43.8 us -> 38.6 us (0.88)
  local copies, waits for them, and re-layouts: 6.75 us -> 3.97 us
  Pallas kernels: 36.8 us -> 34.5 us
    unnamed x9 -> x1, local copies, waits for them, and re-layouts: 6.75 us -> 3.97 us
    pallas_call x1, Pallas kernels: 36.8 us -> 34.5 us  [per_device(): pl.pallas_call(functools.partial(kernel, sizes), out_shape=jax.ShapeDtype...]
where the time goes in v2:
time: 38.6 us; the launch traced here: 38.5 us
  Pallas kernels  34.5 us (89%)
  local copies, waits for them, and re-layouts  3.97 us (10%)
    pallas_call x1, Pallas kernels, per_device(): pl.pallas_call(functools.partial(kernel, sizes), out_shape=jax.ShapeDtype...  34.5 us
    unnamed x1, local copies, waits for them, and re-layouts  3.97 us

profile of v2, /device:TPU:0, one launch (start us, length us, event | category | flops | bytes accessed | tf_op | source)
XLA Modules:
  0.0 38.5 jit_solution(1897063240186434873)
XLA Ops:
  0.0 34.5 %shard_map.46 = f32[4,24,32,256]{3,2,1,0:T(8,128)} custom-call(f32[4,24,32,256]{3,2,1,0:T(8,128)} %state.1, f32[2,24,32,256]{3,2,1,0:T(8,128)} %mixing.1, s32[128,512]{1,0:T(8,128)} %dep_any.1, f32[2,32,256]{2,1,0:T(8,128)} %wind_any.1), custom_call_target="tpu_custom_call" | custom-call | flops 47185920 | bytes 7864320 | tf_op jit(solution)/shard_map/pallas_call | solution.py:601
  34.5 4.0 %copy.6 = f32[4,24,32,256]{3,2,1,0:T(8,128)} copy(f32[4,24,32,256]{3,2,1,0:T(8,128)} %shard_map.46) | data formatting | bytes 6291456

commit v3 on v2

--- a/solution.py
+++ b/solution.py
@@ -21,10 +21,10 @@
 
 def kernel(
     sizes, state, mixing, dep_any, wind_any, out,
-    dep_ref, wind_ref, st, mx, fr, rat, inv, take, take_w, via, w_last, hx_src, hx, hy_src, hy, south_flux, edge_p,
+    dep_ref, wind_ref, st, mx, fr, rat, inv, take, take_w, via, w_last, hx_src, hx, hv_src, hv, hy_src, hy, south_flux, edge_p,
     s_src, s_in, s_acc, h_src, h_in, h_acc,
     c_out, c_in, mh, h_out, r_in, k_in, k_out, k_a, k_b, d_last,
-    dep_sem, wind_sem, st_sem, mx_sem, out_sem, hx_send, hx_recv, hy_send, hy_recv,
+    dep_sem, wind_sem, st_sem, mx_sem, out_sem, hx_send, hx_recv, hv_send, hv_recv, hy_send, hy_recv,
     s_send, s_recv, h_send, h_recv, c_send, c_recv, m_send, m_recv, r_send, r_recv, x_send,
 ):
     gx_n, gy_n, gz_n = sizes
@@ -68,13 +68,45 @@
         pl.semaphore_signal(barrier, inc=1, device_id={"gy": iy - 1}, device_id_type=MESH)
 
     greeted = 2 + (gz_n - 1) + jnp.where(has_north, 1, 0) + jnp.where(has_south, 1, 0)
-    pl.semaphore_wait(barrier, greeted)
 
     def remote(src, dst, send, recv, **device):
         return pltpu.make_async_remote_copy(
             src_ref=src, dst_ref=dst, send_sem=send, recv_sem=recv, device_id=device, device_id_type=MESH
         )
 
+    lane = lax.broadcasted_iota(jnp.int32, (cols, 128), 1)
+    lane_wide = lax.broadcasted_iota(jnp.int32, (cols, rows), 1)
+
+    part = levels // 2
+
+    def rows_out(ch):
+        def one(i, carry):
+            k = first + step * (ch * part + i)
+            for f in range(3):
+                hx_src[0, ch, f, pl.ds(i, 1), :] = st[f, k, cols - 1:cols, :]
+                hx_src[1, ch, f, pl.ds(i, 1), :] = st[f, k, 0:1, :]
+            return carry
+
+        lax.fori_loop(0, part, one, 0)
+
+    x_copies = [
+        [
+            remote(hx_src.at[0, ch], hx.at[0, ch], hx_send.at[0, ch], hx_recv.at[0, ch], gx=east),
+            remote(hx_src.at[1, ch], hx.at[1, ch], hx_send.at[1, ch], hx_recv.at[1, ch], gx=west),
+        ]
+        for ch in range(2)
+    ]
+    v_copies = [
+        remote(hv_src.at[0], hv.at[0], hv_send.at[0], hv_recv.at[0], gx=east),
+        remote(hv_src.at[1], hv.at[1], hv_send.at[1], hv_recv.at[1], gx=west),
+    ]
+    for copy in loads[:3]:
+        copy.wait()
+    rows_out(0)
+    pl.semaphore_wait(barrier, greeted)
+    for copy in x_copies[0]:
+        copy.start()
+
     def mixing_copy(target):
         return remote(mixing.at[:, levels - 1], mh, m_send, m_recv, gz=target)
 
@@ -84,25 +116,7 @@
     def _():
         mixing_copy(z + 1).start()
 
-    lane = lax.broadcasted_iota(jnp.int32, (cols, 128), 1)
-    lane_wide = lax.broadcasted_iota(jnp.int32, (cols, rows), 1)
-
-    for copy in loads:
-        copy.wait()
-
-    def rows_out(k, carry):
-        for f in range(4):
-            hx_src[0, f, pl.ds(k, 1), :] = st[f, k, cols - 1:cols, :]
-            hx_src[1, f, pl.ds(k, 1), :] = st[f, k, 0:1, :]
-        return carry
-
-    lax.fori_loop(0, levels, rows_out, 0)
-    x_copies = [
-        remote(hx_src.at[0], hx.at[0], hx_send.at[0], hx_recv.at[0], gx=east),
-        remote(hx_src.at[1], hx.at[1], hx_send.at[1], hx_recv.at[1], gx=west),
-    ]
-    for copy in x_copies:
-        copy.start()
+    loads[3].wait()
 
     y_copies = [
         remote(hy_src.at[0], hy.at[0], hy_send.at[0], hy_recv.at[0], gy=lax.rem(iy + 1, gy_n)),
@@ -134,6 +148,19 @@
             for f in range(4):
                 hy_src[side, f] = zero
                 hy[absent_in, f] = zero
+
+    rows_out(1)
+    for copy in x_copies[1]:
+        copy.start()
+
+    def v_rows(k, carry):
+        hv_src[0, pl.ds(k, 1), :] = st[3, k, cols - 1:cols, :]
+        hv_src[1, pl.ds(k, 1), :] = st[3, k, 0:1, :]
+        return carry
+
+    lax.fori_loop(0, levels, v_rows, 0)
+    for copy in v_copies:
+        copy.start()
 
     load_dep.wait()
     start_x = pl.multiple_of(ix * cols, cols)
@@ -245,7 +272,7 @@
         w_last[...] = jnp.zeros((cols, rows), F32)
         coefficients()
 
-    for copy in x_copies:
+    for copy in x_copies[0]:
         copy.wait_recv()
 
     @pl.when(has_south)
@@ -256,16 +283,63 @@
     def _():
         y_copies[1].wait_recv()
 
-    def total_rows(k, totals):
+    lane_level = jnp.where(lane < levels, base + lane, 1 << 20)
+
+    wet_s = lane_level < jnp.minimum(dep_s, dep[:, 0:1])
+
+    def takes(both, wet):
+        vel = both * jnp.where(wet, 0.125, 0.0).astype(F32)
+        near = jnp.maximum(vel, 0.0) + jnp.where(wet, 0.08, 0.0).astype(F32)
+        return near, vel - near
+
+    take_s, take_n = takes(hy[0, 3] + hy_src[1, 3], wet_s)
+    for f in range(4):
+        south_flux[f] = take_s * hy[0, f] + take_n * hy_src[1, f]
+
+    def moved_of(f, k, c, w, e, c_e, c_n, ax, bx, ay, by, aw, bw):
+        flux_x = ax * c + bx * c_e
+        flux_y = ay * c + by * c_n
+        flux_w = from_west(flux_x, aw * w + bw * c[0:1])
+        flux_s = from_south(flux_y, pltpu.roll(south_flux[f], lax.rem(128 - k, 128), 1))
+        return c - (flux_x - flux_w + flux_y - flux_s)
+
+    def advance_tracers(t, carry, ch):
+        k = first + step * t
+        ct = pl.ds(t - ch * part, 1)
+        kg = base + k
         at = pl.ds(k, 1)
-        w = density_of(hx[0, 0, at, :], hx[0, 1, at, :]) * as_float(base + k < dep_w)
-        e = density_of(hx[1, 0, at, :], hx[1, 1, at, :]) * as_float(base + k < dep_e)
+        to_north = 127 - k
+        u, v = st[2, k], st[3, k]
+        ax, bx = takes(u + from_east(u, hx[1, ch, 2, ct, :]), kg < least_e)
+        ay, by = takes(v + from_north(v, pltpu.roll(hy[1, 3], to_north, 1)), kg < least_n)
+        aw, bw = takes(hx[0, ch, 2, ct, :] + u[0:1], kg < least_w)
+        take[0, k], take[1, k], take[2, k], take[3, k] = ax, bx, ay, by
+        take_w[0, at, :], take_w[1, at, :] = aw, bw
+        wet = as_float(kg < dep)
+        for f in range(2):
+            c, w, e = st[f, k], hx[0, ch, f, ct, :], hx[1, ch, f, ct, :]
+            c_n = from_north(c, pltpu.roll(hy[1, f], to_north, 1))
+            fr[f, k] = moved_of(f, k, c, w, e, from_east(c, e), c_n, ax, bx, ay, by, aw, bw) * wet
+        return carry
+
+    lax.fori_loop(0, part, functools.partial(advance_tracers, ch=0), 0)
+
+    for copy in x_copies[1]:
+        copy.wait_recv()
+
+    def where_rows(t):
+        ch = jnp.where(t < part, 0, 1)
+        return ch, pl.ds(t - ch * part, 1)
+
+    def total_rows(t, totals):
+        ch, at = where_rows(t)
+        k = first + step * t
+        w = density_of(hx[0, ch, 0, at, :], hx[0, ch, 1, at, :]) * as_float(base + k < dep_w)
+        e = density_of(hx[1, ch, 0, at, :], hx[1, ch, 1, at, :]) * as_float(base + k < dep_e)
         return totals[0] + w, totals[1] + e
 
     row_zero = jnp.zeros((1, rows), F32)
     tot_w, tot_e = lax.fori_loop(0, levels, total_rows, (row_zero, row_zero))
-
-    lane_level = jnp.where(lane < levels, base + lane, 1 << 20)
 
     def running(dens):
         sh = 1
@@ -281,9 +355,9 @@
     tot_s = jnp.sum(dens_s, axis=1, keepdims=True)
     h_src[0:cols, :] = jnp.where(lane == 0, tot_s, jnp.where(lane == 1, tot_n, 0.0))
     for b in range(blocks):
-        part = slice(b * 128, b * 128 + 128)
+        piece = slice(b * 128, b * 128 + 128)
         at = cols + 8 * b
-        h_src[at:at + 8, :] = jnp.concatenate([tot_w[:, part], tot_e[:, part], jnp.zeros((6, 128), F32)], axis=0)
+        h_src[at:at + 8, :] = jnp.concatenate([tot_w[:, piece], tot_e[:, piece], jnp.zeros((6, 128), F32)], axis=0)
 
     for d in range(1, gz_n):
 
@@ -291,44 +365,7 @@
         def _(d=d):
             h_copy(d, z).start()
 
-    mask_s = as_float(lane_level < jnp.minimum(dep_s, dep[:, 0:1]))
-
-    def takes(vel, mask):
-        return 0.25 * jnp.maximum(vel, 0.0) + 0.08 * mask, 0.25 * jnp.minimum(vel, 0.0) - 0.08 * mask
-
-    take_s, take_n = takes(0.5 * (hy[0, 3] + hy_src[1, 3]) * mask_s, mask_s)
-    for f in range(4):
-        south_flux[f] = take_s * hy[0, f] + take_n * hy_src[1, f]
-
-    def moved_of(f, k, c, w, e, c_e, c_n, ax, bx, ay, by, aw, bw):
-        flux_x = ax * c + bx * c_e
-        flux_y = ay * c + by * c_n
-        flux_w = from_west(flux_x, aw * w + bw * c[0:1])
-        flux_s = from_south(flux_y, pltpu.roll(south_flux[f], lax.rem(128 - k, 128), 1))
-        return c - (flux_x - flux_w + flux_y - flux_s)
-
-    def advance_tracers(t, carry):
-        k = first + step * t
-        kg = base + k
-        at = pl.ds(k, 1)
-        to_north = 127 - k
-        mask_x = as_float(kg < least_e)
-        mask_y = as_float(kg < least_n)
-        mask_w = as_float(kg < least_w)
-        u, v = st[2, k], st[3, k]
-        ax, bx = takes(0.5 * (u + from_east(u, hx[1, 2, at, :])) * mask_x, mask_x)
-        ay, by = takes(0.5 * (v + from_north(v, pltpu.roll(hy[1, 3], to_north, 1))) * mask_y, mask_y)
-        aw, bw = takes(0.5 * (hx[0, 2, at, :] + u[0:1]) * mask_w, mask_w)
-        take[0, k], take[1, k], take[2, k], take[3, k] = ax, bx, ay, by
-        take_w[0, at, :], take_w[1, at, :] = aw, bw
-        wet = as_float(kg < dep)
-        for f in range(2):
-            c, w, e = st[f, k], hx[0, f, at, :], hx[1, f, at, :]
-            c_n = from_north(c, pltpu.roll(hy[1, f], to_north, 1))
-            fr[f, k] = moved_of(f, k, c, w, e, from_east(c, e), c_n, ax, bx, ay, by, aw, bw) * wet
-        return carry
-
-    lax.fori_loop(0, levels, advance_tracers, 0)
+    lax.fori_loop(part, levels, functools.partial(advance_tracers, ch=1), 0)
 
     @pl.when(has_out)
     def _():
@@ -391,7 +428,7 @@
     edge_p[0] = h_acc[0:cols, 1:2] + running(dens_n) - 0.5 * dens_n
     p_s = h_acc[0:cols, 0:1] + running(dens_s) - 0.5 * dens_s
     p_o = s_acc[:, 0:1] + running(dens_o) - 0.5 * dens_o
-    edge_p[1] = mask_s * (p_o - p_s)
+    edge_p[1] = as_float(wet_s) * (p_o - p_s)
 
     sign = jnp.where(down, 1.0, -1.0).astype(F32)
     own = jnp.where(down, 0.0, 1.0).astype(F32)
@@ -404,6 +441,8 @@
     run_e = wide_row(h_acc, 1) + own * wide_row(h_src, 1)
     coriolis = 0.3 * (0.5 + ((start_y + lane_wide).astype(F32) + 0.5) / total_y)
     load_wind.wait()
+    for copy in v_copies:
+        copy.wait_recv()
 
     def advance(t, carry):
         run, run_w, run_e, g_u, g_v = carry
@@ -413,8 +452,9 @@
         to_north = 127 - k
         to_south = lax.rem(128 - k, 128)
         c = [st[f, k] for f in range(4)]
-        w = [hx[0, f, at, :] for f in range(4)]
-        e = [hx[1, f, at, :] for f in range(4)]
+        ch, ct = where_rows(t)
+        w = [hx[0, ch, f, ct, :] for f in range(3)] + [hv[0, at, :]]
+        e = [hx[1, ch, f, ct, :] for f in range(3)] + [hv[1, at, :]]
         wet = as_float(kg < dep)
         mask_x = as_float(kg < least_e)
         mask_y = as_float(kg < least_n)
@@ -510,11 +550,14 @@
     @pl.when(has_out)
     def _():
         backward_tracers()
-        for f in (2, 3):
+
+    for f in (2, 3):
+
+        @pl.when(has_out)
+        def _(f=f):
             wait_in(0, f)
             fr[f, final] = fr[f, final] + w_last[...] * r_in[0, f]
 
-    for f in (2, 3):
         h_out[f] = k_out[1] * fr[f, final]
         in_copies[f].start()
 
@@ -524,18 +567,17 @@
 
     for f in (2, 3):
         wait_in(1, f)
-        fr[f, final] = k_a[1] * fr[f, final] + k_b[1] * r_in[1, f]
-
-    def backward(t, x):
-        k = final - step * t
-        ratio, over, add = rat[1, k + step], inv[1, k], via[k]
-        new = tuple(over * fr[2 + i, k] + ratio * x[i] + add * r_in[0, 2 + i] for i in range(2))
-        for i in range(2):
-            fr[2 + i, k] = new[i]
-        return new
-
-    lax.fori_loop(1, levels, backward, (fr[2, final], fr[3, final]))
-    for f in (2, 3):
+        came = r_in[0, f]
+        x = k_a[1] * fr[f, final] + k_b[1] * r_in[1, f]
+        fr[f, final] = x
+
+        def backward(t, x, f=f, came=came):
+            k = final - step * t
+            x = inv[1, k] * fr[f, k] + rat[1, k + step] * x + via[k] * came
+            fr[f, k] = x
+            return x
+
+        lax.fori_loop(1, levels, backward, x)
 
         @pl.when(has_out)
         def _(f=f):
@@ -543,7 +585,7 @@
 
         stores[f].start()
 
-    for copy in x_copies:
+    for copy in x_copies[0] + x_copies[1] + v_copies:
         copy.wait_send()
     for side, present in ((0, has_north), (1, has_south)):
 
@@ -571,6 +613,26 @@
             out_copies[f].wait_send()
 
         stores[f].wait()
+
+
+def place(source, target, held, in_sem, out_sem):
+    part = source.shape[1] // 2
+    pieces = [(f, h) for f in range(4) for h in range(2)]
+    ins = [
+        pltpu.make_async_copy(source.at[f, pl.ds(h * part, part)], held.at[f, pl.ds(h * part, part)], in_sem.at[f, h])
+        for f, h in pieces
+    ]
+    outs = [
+        pltpu.make_async_copy(held.at[f, pl.ds(h * part, part)], target.at[f, pl.ds(h * part, part)], out_sem.at[f, h])
+        for f, h in pieces
+    ]
+    for copy in ins:
+        copy.start()
+    for arrived, leaving in zip(ins, outs):
+        arrived.wait()
+        leaving.start()
+    for copy in outs:
+        copy.wait()
 
 
 def per_device(sizes, state, mixing, depth_levels, wind):
@@ -589,16 +651,17 @@
         vmem(4, levels, *tile), vmem(2, levels, *tile), vmem(4, levels, *tile),
         vmem(2, levels, *tile), vmem(2, levels, *tile),
         vmem(4, levels, *tile), vmem(2, levels, rows), vmem(levels, *tile), vmem(*tile),
-        vmem(2, 4, levels, rows), vmem(2, 4, levels, rows), vmem(2, 4, cols, 128), vmem(2, 4, cols, 128),
+        vmem(2, 2, 3, levels // 2, rows), vmem(2, 2, 3, levels // 2, rows), vmem(2, levels, rows), vmem(2, levels, rows),
+        vmem(2, 4, cols, 128), vmem(2, 4, cols, 128),
         vmem(4, cols, 128), vmem(2, cols, 128),
         vmem(*tile), vmem(earlier, *tile), vmem(*tile),
         vmem(h_rows, 128), vmem(earlier, h_rows, 128), vmem(h_rows, 128),
         vmem(2, *tile), vmem(2, 2, *tile), vmem(2, *tile), vmem(4, *tile), vmem(2, 4, *tile),
         vmem(2, *tile), vmem(2, *tile), vmem(2, *tile), vmem(2, *tile), vmem(2, *tile),
-        one, one, dma(4), one, dma(4), dma(2), dma(2), dma(2), dma(2),
+        one, one, dma(4), one, dma(4), dma(2, 2), dma(2, 2), dma(2), dma(2), dma(2), dma(2),
         dma(earlier), dma(earlier), dma(earlier), dma(earlier), one, dma(2), one, one, dma(4), dma(2, 4), dma(4),
     ]
-    return pl.pallas_call(
+    solved = pl.pallas_call(
         functools.partial(kernel, sizes),
         out_shape=jax.ShapeDtypeStruct(state.shape, F32),
         in_specs=[any_spec] * 4,
@@ -609,6 +672,15 @@
         ),
         cost_estimate=pl.CostEstimate(flops=state.size * 60, bytes_accessed=state.size * 10, transcendentals=0),
     )(state, mixing, depth_levels, wind)
+    return pl.pallas_call(
+        place,
+        out_shape=jax.ShapeDtypeStruct(state.shape, F32),
+        in_specs=[any_spec],
+        out_specs=any_spec,
+        scratch_shapes=[vmem(*state.shape), dma(4, 2), dma(4, 2)],
+        compiler_params=pltpu.CompilerParams(vmem_limit_bytes=60 * 1024 * 1024),
+        cost_estimate=pl.CostEstimate(flops=0, bytes_accessed=state.size * 8, transcendentals=0),
+    )(solved)
 
 
 def solution(mesh):

time: 38.6 us -> 37.2 us (0.964)
  local copies, waits for them, and re-layouts: 3.97 us -> 0 us
  Pallas kernels: 34.5 us -> 37 us
    unnamed x1 -> x0, local copies, waits for them, and re-layouts: 3.97 us -> none
    pallas_call x0 -> x1, Pallas kernels: none -> 2.79 us  [per_device(): pl.pallas_call(place, out_shape=jax.ShapeDtypeStruct(state.shape, F32), i...]
where the time goes in v3:
time: 37.2 us; the launch traced here: 37 us
  Pallas kernels  37 us (99%)
    pallas_call x1, Pallas kernels, per_device(): pl.pallas_call(functools.partial(kernel, sizes), out_shape=jax.ShapeDtype...  34.2 us
    pallas_call x1, Pallas kernels, per_device(): pl.pallas_call(place, out_shape=jax.ShapeDtypeStruct(state.shape, F32), i...  2.79 us

profile of v3, /device:TPU:0, one launch (start us, length us, event | category | flops | bytes accessed | tf_op | source)
XLA Modules:
  0.0 37.0 jit_solution(17231296026508963487)
XLA Ops:
  0.0 34.2 %shard_map.46.source = f32[4,24,32,256]{3,2,1,0:T(8,128)} custom-call(f32[4,24,32,256]{3,2,1,0:T(8,128)} %state.1, f32[2,24,32,256]{3,2,1,0:T(8,128)} %mixing.1, s32[128,512]{1,0:T(8,128)} %dep_any.1, f32[2,32,256]{2,1,0:T(8,128)} %wind_any.1), custom_call_target="tpu_custom_call" | custom-call | flops 47185920 | bytes 7864320 | tf_op jit(solution)/shard_map/pallas_call | solution.py:664
  34.3 2.8 %shard_map.47 = f32[4,24,32,256]{3,2,1,0:T(8,128)} custom-call(f32[4,24,32,256]{3,2,1,0:T(8,128)} %shard_map.46.source), custom_call_target="tpu_custom_call" | custom-call | bytes 6291456 | tf_op jit(solution)/shard_map/pallas_call | solution.py:675

commit v4 on v3

--- a/solution.py
+++ b/solution.py
@@ -21,7 +21,7 @@
 
 def kernel(
     sizes, state, mixing, dep_any, wind_any, out,
-    dep_ref, wind_ref, st, mx, fr, rat, inv, take, take_w, via, w_last, hx_src, hx, hv_src, hv, hy_src, hy, south_flux, edge_p,
+    dep_ref, wind_ref, st, mx, fr, rat, inv, take, take_w, via, w_last, depths, run_ref, g_ref, hx_src, hx, hv_src, hv, hy_src, hy, south_flux, edge_p,
     s_src, s_in, s_acc, h_src, h_in, h_acc,
     c_out, c_in, mh, h_out, r_in, k_in, k_out, k_a, k_b, d_last,
     dep_sem, wind_sem, st_sem, mx_sem, out_sem, hx_send, hx_recv, hv_send, hv_recv, hy_send, hy_recv,
@@ -75,7 +75,6 @@
         )
 
     lane = lax.broadcasted_iota(jnp.int32, (cols, 128), 1)
-    lane_wide = lax.broadcasted_iota(jnp.int32, (cols, rows), 1)
 
     part = levels // 2
 
@@ -197,6 +196,7 @@
     least_e = jnp.minimum(dep, from_east(dep, dep_e))
     least_n = jnp.minimum(dep, from_north(dep, jnp.broadcast_to(dep_n, (cols, 128))))
     least_w = jnp.minimum(dep[0:1], dep_w)
+    depths[0], depths[1], depths[2] = dep, least_e, least_n
 
     def total_one(k, total):
         return total + density_of(st[0, k], st[1, k]) * as_float(base + k < dep)
@@ -296,11 +296,49 @@
     for f in range(4):
         south_flux[f] = take_s * hy[0, f] + take_n * hy_src[1, f]
 
-    def moved_of(f, k, c, w, e, c_e, c_n, ax, bx, ay, by, aw, bw):
+    spans = [slice(8 * i, 8 * i + 8) for i in range(tiles)]
+    tile_lane = lax.broadcasted_iota(jnp.int32, (8, 128), 1)
+
+    def halves(array):
+        return [array[:, 128 * b:128 * b + 128] for b in range(blocks)]
+
+    def tile_north(array, block):
+        turned = [pltpu.roll(a, 127, 1) for a in halves(array)] + [block]
+        return jnp.concatenate([jnp.where(tile_lane == 127, turned[b + 1], turned[b]) for b in range(blocks)], axis=1)
+
+    def tile_south(array, block):
+        turned = [block] + [pltpu.roll(a, 1, 1) for a in halves(array)]
+        return jnp.concatenate([jnp.where(tile_lane == 0, turned[b], turned[b + 1]) for b in range(blocks)], axis=1)
+
+    class Easts:
+        def __init__(self, get, row):
+            self.get, self.row = get, row
+            self.ahead = get(0)
+            self.turned = pltpu.roll(self.ahead, 7, 0)
+
+        def next(self, i):
+            here, turned = self.ahead, self.turned
+            if i + 1 < tiles:
+                self.ahead = self.get(i + 1)
+                self.turned = pltpu.roll(self.ahead, 7, 0)
+            else:
+                self.turned = self.row
+            return here, jnp.where(tile_row == 7, self.turned, turned)
+
+    class Wests:
+        def __init__(self, row):
+            self.turned = row
+
+        def next(self, tile):
+            before, self.turned = self.turned, pltpu.roll(tile, 1, 0)
+            return jnp.where(tile_row == 0, before, self.turned)
+
+    def moved_of(f, i, c, c_e, wests, to_north, to_south, ax, bx, ay, by):
+        c_n = tile_north(c, pltpu.roll(hy[1, f, spans[i]], to_north, 1))
         flux_x = ax * c + bx * c_e
         flux_y = ay * c + by * c_n
-        flux_w = from_west(flux_x, aw * w + bw * c[0:1])
-        flux_s = from_south(flux_y, pltpu.roll(south_flux[f], lax.rem(128 - k, 128), 1))
+        flux_w = wests.next(flux_x)
+        flux_s = tile_south(flux_y, pltpu.roll(south_flux[f, spans[i]], to_south, 1))
         return c - (flux_x - flux_w + flux_y - flux_s)
 
     def advance_tracers(t, carry, ch):
@@ -308,18 +346,22 @@
         ct = pl.ds(t - ch * part, 1)
         kg = base + k
         at = pl.ds(k, 1)
-        to_north = 127 - k
-        u, v = st[2, k], st[3, k]
-        ax, bx = takes(u + from_east(u, hx[1, ch, 2, ct, :]), kg < least_e)
-        ay, by = takes(v + from_north(v, pltpu.roll(hy[1, 3], to_north, 1)), kg < least_n)
-        aw, bw = takes(hx[0, ch, 2, ct, :] + u[0:1], kg < least_w)
-        take[0, k], take[1, k], take[2, k], take[3, k] = ax, bx, ay, by
+        to_north, to_south = 127 - k, lax.rem(128 - k, 128)
+        aw, bw = takes(hx[0, ch, 2, ct, :] + st[2, k, 0:1, :], kg < least_w)
         take_w[0, at, :], take_w[1, at, :] = aw, bw
-        wet = as_float(kg < dep)
-        for f in range(2):
-            c, w, e = st[f, k], hx[0, ch, f, ct, :], hx[1, ch, f, ct, :]
-            c_n = from_north(c, pltpu.roll(hy[1, f], to_north, 1))
-            fr[f, k] = moved_of(f, k, c, w, e, from_east(c, e), c_n, ax, bx, ay, by, aw, bw) * wet
+        east_of = [Easts(lambda i, f=f: st[f, k, spans[i], :], hx[1, ch, f, ct, :]) for f in range(3)]
+        west_of = [Wests(aw * hx[0, ch, f, ct, :] + bw * st[f, k, 0:1, :]) for f in range(2)]
+        for i in range(tiles):
+            sp = spans[i]
+            u, u_e = east_of[2].next(i)
+            v = st[3, k, sp, :]
+            ax, bx = takes(u + u_e, kg < depths[1, sp])
+            ay, by = takes(v + tile_north(v, pltpu.roll(hy[1, 3, sp], to_north, 1)), kg < depths[2, sp])
+            take[0, k, sp, :], take[1, k, sp, :], take[2, k, sp, :], take[3, k, sp, :] = ax, bx, ay, by
+            wet = as_float(kg < depths[0, sp])
+            for f in range(2):
+                c, c_e = east_of[f].next(i)
+                fr[f, k, sp, :] = moved_of(f, i, c, c_e, west_of[f], to_north, to_south, ax, bx, ay, by) * wet
         return carry
 
     lax.fori_loop(0, part, functools.partial(advance_tracers, ch=0), 0)
@@ -436,54 +478,65 @@
     def wide_row(ref, r):
         return jnp.concatenate([ref[cols + 8 * b + r:cols + 8 * b + r + 1, :] for b in range(blocks)], axis=1)
 
-    run = s_acc[...] + own * s_src[...]
+    run_ref[...] = s_acc[...] + own * s_src[...]
+    g_ref[...] = jnp.zeros_like(g_ref)
     run_w = wide_row(h_acc, 0) + own * wide_row(h_src, 0)
     run_e = wide_row(h_acc, 1) + own * wide_row(h_src, 1)
-    coriolis = 0.3 * (0.5 + ((start_y + lane_wide).astype(F32) + 0.5) / total_y)
+    row_lane = lax.broadcasted_iota(jnp.int32, (8, rows), 1)
+    coriolis = 0.3 * (0.5 + ((start_y + row_lane).astype(F32) + 0.5) / total_y)
     load_wind.wait()
     for copy in v_copies:
         copy.wait_recv()
 
     def advance(t, carry):
-        run, run_w, run_e, g_u, g_v = carry
+        run_w, run_e = carry
         k = first + step * t
         kg = base + k
         at = pl.ds(k, 1)
-        to_north = 127 - k
-        to_south = lax.rem(128 - k, 128)
-        c = [st[f, k] for f in range(4)]
+        to_north, to_south = 127 - k, lax.rem(128 - k, 128)
         ch, ct = where_rows(t)
         w = [hx[0, ch, f, ct, :] for f in range(3)] + [hv[0, at, :]]
         e = [hx[1, ch, f, ct, :] for f in range(3)] + [hv[1, at, :]]
-        wet = as_float(kg < dep)
-        mask_x = as_float(kg < least_e)
-        mask_y = as_float(kg < least_n)
-        mask_w = as_float(kg < least_w)
-        coefs = (take[0, k], take[1, k], take[2, k], take[3, k], take_w[0, at, :], take_w[1, at, :])
-        moved = [None, None]
-        for f in (2, 3):
-            c_n = from_north(c[f], pltpu.roll(hy[1, f], to_north, 1))
-            moved.append(moved_of(f, k, c[f], w[f], e[f], from_east(c[f], e[f]), c_n, *coefs))
-        dens = density_of(c[0], c[1]) * wet
+        aw, bw = take_w[0, at, :], take_w[1, at, :]
         dens_w = density_of(w[0], w[1]) * as_float(kg < dep_w)
         dens_e = density_of(e[0], e[1]) * as_float(kg < dep_e)
-        p = run + (0.5 * sign) * dens
         p_w = run_w + (0.5 * sign) * dens_w
         p_e = run_e + (0.5 * sign) * dens_e
-        g_x = mask_x * (from_east(p, p_e) - p)
-        g_y = mask_y * (from_north(p, pltpu.roll(edge_p[0], to_north, 1)) - p)
-        g_x = g_x + from_west(g_x, mask_w * (p[0:1] - p_w))
-        g_y = g_y + from_south(g_y, pltpu.roll(edge_p[1], to_south, 1))
         top = jnp.where(kg == 0, 1.0, 0.0).astype(F32)
-        ratio = rat[1, k]
-        g_u = (moved[2] + coriolis * c[3] - 0.015 * g_x + top * wind_ref[0]) * wet + ratio * g_u
-        g_v = (moved[3] - coriolis * c[2] - 0.015 * g_y + top * wind_ref[1]) * wet + ratio * g_v
-        fr[2, k] = g_u
-        fr[3, k] = g_v
-        return run + sign * dens, run_w + sign * dens_w, run_e + sign * dens_e, g_u, g_v
-
-    wide_zero = jnp.zeros((cols, rows), F32)
-    lax.fori_loop(0, levels, advance, (run, run_w, run_e, wide_zero, wide_zero))
+
+        def pressure(i):
+            sp = spans[i]
+            dens = density_of(st[0, k, sp, :], st[1, k, sp, :]) * as_float(kg < depths[0, sp])
+            run = run_ref[sp, :]
+            run_ref[sp, :] = run + sign * dens
+            return run + (0.5 * sign) * dens
+
+        east_p = Easts(pressure, p_e)
+        west_p = Wests(as_float(kg < least_w) * (east_p.ahead[0:1] - p_w))
+        east_of = [Easts(lambda i, f=f: st[f, k, spans[i], :], e[f]) for f in (2, 3)]
+        west_of = [Wests(aw * w[f] + bw * st[f, k, 0:1, :]) for f in (2, 3)]
+        for i in range(tiles):
+            sp = spans[i]
+            coefs = [take[n, k, sp, :] for n in range(4)]
+            wet = as_float(kg < depths[0, sp])
+            p, p_east = east_p.next(i)
+            g_x = as_float(kg < depths[1, sp]) * (p_east - p)
+            g_y = as_float(kg < depths[2, sp]) * (tile_north(p, pltpu.roll(edge_p[0, sp], to_north, 1)) - p)
+            g_x = g_x + west_p.next(g_x)
+            g_y = g_y + tile_south(g_y, pltpu.roll(edge_p[1, sp], to_south, 1))
+            (u, u_e), (v, v_e) = east_of[0].next(i), east_of[1].next(i)
+            ratio = rat[1, k, sp, :]
+            new_u = moved_of(2, i, u, u_e, west_of[0], to_north, to_south, *coefs)
+            new_u = (new_u + coriolis * v - 0.015 * g_x + top * wind_ref[0, sp, :]) * wet + ratio * g_ref[0, sp, :]
+            g_ref[0, sp, :] = new_u
+            fr[2, k, sp, :] = new_u
+            new_v = moved_of(3, i, v, v_e, west_of[1], to_north, to_south, *coefs)
+            new_v = (new_v - coriolis * u - 0.015 * g_y + top * wind_ref[1, sp, :]) * wet + ratio * g_ref[1, sp, :]
+            g_ref[1, sp, :] = new_v
+            fr[3, k, sp, :] = new_v
+        return run_w + sign * dens_w, run_e + sign * dens_e
+
+    lax.fori_loop(0, levels, advance, (run_w, run_e))
 
     @pl.when(mid)
     def _():
@@ -651,6 +704,7 @@
         vmem(4, levels, *tile), vmem(2, levels, *tile), vmem(4, levels, *tile),
         vmem(2, levels, *tile), vmem(2, levels, *tile),
         vmem(4, levels, *tile), vmem(2, levels, rows), vmem(levels, *tile), vmem(*tile),
+        pltpu.VMEM((3, *tile), jnp.int32), vmem(*tile), vmem(2, *tile),
         vmem(2, 2, 3, levels // 2, rows), vmem(2, 2, 3, levels // 2, rows), vmem(2, levels, rows), vmem(2, levels, rows),
         vmem(2, 4, cols, 128), vmem(2, 4, cols, 128),
         vmem(4, cols, 128), vmem(2, cols, 128),

time: 37.2 us -> 37 us (level)
  no operation moved by 1% of the time
where the time goes in v4:
time: 37 us; the launch traced here: 36.9 us
  Pallas kernels  36.9 us (100%)
    pallas_call x1, Pallas kernels, per_device(): pl.pallas_call(functools.partial(kernel, sizes), out_shape=jax.ShapeDtype...  34.1 us
    pallas_call x1, Pallas kernels, per_device(): pl.pallas_call(place, out_shape=jax.ShapeDtypeStruct(state.shape, F32), i...  2.79 us

profile of v4, /device:TPU:0, one launch (start us, length us, event | category | flops | bytes accessed | tf_op | source)
XLA Modules:
  0.0 36.9 jit_solution(8902493532070140973)
XLA Ops:
  0.0 34.1 %shard_map.46.source = f32[4,24,32,256]{3,2,1,0:T(8,128)} custom-call(f32[4,24,32,256]{3,2,1,0:T(8,128)} %state.1, f32[2,24,32,256]{3,2,1,0:T(8,128)} %mixing.1, s32[128,512]{1,0:T(8,128)} %dep_any.1, f32[2,32,256]{2,1,0:T(8,128)} %wind_any.1), custom_call_target="tpu_custom_call" | custom-call | flops 47185920 | bytes 7864320 | tf_op jit(solution)/shard_map/pallas_call | solution.py:718
  34.1 2.8 %shard_map.47 = f32[4,24,32,256]{3,2,1,0:T(8,128)} custom-call(f32[4,24,32,256]{3,2,1,0:T(8,128)} %shard_map.46.source), custom_call_target="tpu_custom_call" | custom-call | bytes 6291456 | tf_op jit(solution)/shard_map/pallas_call | solution.py:729

commit v5 on v4

--- a/solution.py
+++ b/solution.py
@@ -395,11 +395,17 @@
     dens_o = density_of(hy_src[1, 0], hy_src[1, 1]) * as_float(lane_level < dep[:, 0:1])
     tot_n = jnp.sum(dens_n, axis=1, keepdims=True)
     tot_s = jnp.sum(dens_s, axis=1, keepdims=True)
-    h_src[0:cols, :] = jnp.where(lane == 0, tot_s, jnp.where(lane == 1, tot_n, 0.0))
-    for b in range(blocks):
-        piece = slice(b * 128, b * 128 + 128)
-        at = cols + 8 * b
-        h_src[at:at + 8, :] = jnp.concatenate([tot_w[:, piece], tot_e[:, piece], jnp.zeros((6, 128), F32)], axis=0)
+    diagonal = lane == lax.broadcasted_iota(jnp.int32, (cols, 128), 0)
+
+    def to_row(column):
+        return jnp.sum(jnp.where(diagonal, column, 0.0), axis=0, keepdims=True)
+
+    def to_column(row):
+        return jnp.sum(jnp.where(diagonal, row, 0.0), axis=1, keepdims=True)
+
+    pieces = [side[:, 128 * b:128 * b + 128] for side in (tot_w, tot_e) for b in range(blocks)]
+    rest = jnp.zeros((h_src.shape[0] - 2 * blocks - 2, 128), F32)
+    h_src[...] = jnp.concatenate(pieces + [to_row(tot_s), to_row(tot_n), rest], axis=0)
 
     for d in range(1, gz_n):
 
@@ -467,8 +473,8 @@
             h_copy(1, p).wait_recv()
             h_acc[...] = h_acc[...] + h_in[p]
 
-    edge_p[0] = h_acc[0:cols, 1:2] + running(dens_n) - 0.5 * dens_n
-    p_s = h_acc[0:cols, 0:1] + running(dens_s) - 0.5 * dens_s
+    edge_p[0] = to_column(h_acc[2 * blocks + 1:2 * blocks + 2, :]) + running(dens_n) - 0.5 * dens_n
+    p_s = to_column(h_acc[2 * blocks:2 * blocks + 1, :]) + running(dens_s) - 0.5 * dens_s
     p_o = s_acc[:, 0:1] + running(dens_o) - 0.5 * dens_o
     edge_p[1] = as_float(wet_s) * (p_o - p_s)
 
@@ -476,7 +482,7 @@
     own = jnp.where(down, 0.0, 1.0).astype(F32)
 
     def wide_row(ref, r):
-        return jnp.concatenate([ref[cols + 8 * b + r:cols + 8 * b + r + 1, :] for b in range(blocks)], axis=1)
+        return jnp.concatenate([ref[r * blocks + b:r * blocks + b + 1, :] for b in range(blocks)], axis=1)
 
     run_ref[...] = s_acc[...] + own * s_src[...]
     g_ref[...] = jnp.zeros_like(g_ref)
@@ -697,7 +703,7 @@
     dma = lambda *shape: pltpu.SemaphoreType.DMA(shape)
     tile = (cols, rows)
     earlier = max(gz_n - 1, 1)
-    h_rows = cols + 8 * blocks
+    h_rows = 8 * pl.cdiv(2 * blocks + 3, 8)
     one = pltpu.SemaphoreType.DMA
     scratch = [
         pltpu.VMEM(depth_levels.shape, jnp.int32), vmem(2, *tile),

time: 37 us -> 36.3 us (0.981)
  Pallas kernels: 36.9 us -> 36.2 us
    pallas_call x1, Pallas kernels: 34.1 us -> 33.4 us  [per_device(): pl.pallas_call(functools.partial(kernel, sizes), out_shape=jax.ShapeDtype...]
where the time goes in v5:
time: 36.3 us; the launch traced here: 36.2 us
  Pallas kernels  36.2 us (100%)
    pallas_call x1, Pallas kernels, per_device(): pl.pallas_call(functools.partial(kernel, sizes), out_shape=jax.ShapeDtype...  33.4 us
    pallas_call x1, Pallas kernels, per_device(): pl.pallas_call(place, out_shape=jax.ShapeDtypeStruct(state.shape, F32), i...  2.79 us

profile of v5, /device:TPU:0, one launch (start us, length us, event | category | flops | bytes accessed | tf_op | source)
XLA Modules:
  0.0 36.2 jit_solution(3271403443942129290)
XLA Ops:
  0.0 33.4 %shard_map.46.source = f32[4,24,32,256]{3,2,1,0:T(8,128)} custom-call(f32[4,24,32,256]{3,2,1,0:T(8,128)} %state.1, f32[2,24,32,256]{3,2,1,0:T(8,128)} %mixing.1, s32[128,512]{1,0:T(8,128)} %dep_any.1, f32[2,32,256]{2,1,0:T(8,128)} %wind_any.1), custom_call_target="tpu_custom_call" | custom-call | flops 47185920 | bytes 7864320 | tf_op jit(solution)/shard_map/pallas_call | solution.py:724
  33.4 2.8 %shard_map.47 = f32[4,24,32,256]{3,2,1,0:T(8,128)} custom-call(f32[4,24,32,256]{3,2,1,0:T(8,128)} %shard_map.46.source), custom_call_target="tpu_custom_call" | custom-call | bytes 6291456 | tf_op jit(solution)/shard_map/pallas_call | solution.py:735
